TPU v7x, 128 devices: a whole 4x4x4 slice. The times are simulated.
128 devices in a mesh: seq: 8 (over y, z_hi), res: 16 (over z_lo, x, core).
Axes of the slice: x: 4, y: 4, z: 4 (z_hi: 2, z_lo: 2; z = z_hi * 2 + z_lo), core: 2. Of those that a mesh axis runs over, the one named last changes fastest.
Arguments:
- tokens: bfloat16 [96, 1024, 768], P('seq', 'res'), may hold values from -8 to 8
- w_query: bfloat16 [768, 768], replicated, may hold values from -0.625 to 0.625
- w_keyval: bfloat16 [768, 1536], replicated, may hold values from -0.21875 to 0.21875
- w_out: bfloat16 [768, 768], replicated, may hold values from -0.21875 to 0.21875
Outputs:
- mixed: float32 [96, 1024, 768], P('seq', 'res')
All inputs are finite; a program needn't handle non-finite values.
Results may differ from a plain program's by a relative error of at most 0.012.
Values may be sent and summed in bfloat16 or wider, within the bound.
A program may use at most 192 MiB of HBM per device.

v0:
```python
import math

import jax
import jax.numpy as jnp
from jax import lax
from jax.sharding import PartitionSpec as P

DH = 64


def softmax_rows(logits):
    largest = jnp.max(logits, axis=-1, keepdims=True)
    weights = jnp.exp(logits - largest)
    return (weights / jnp.sum(weights, axis=-1, keepdims=True)).astype(jnp.bfloat16)


def local(tokens, w_query, w_keyval, w_out):
    seq_dev, res_dev, width = tokens.shape
    head_dim = DH
    heads = width // head_dim
    scale = 1.0 / math.sqrt(head_dim * seq_dev * lax.axis_size("seq"))
    flat = tokens.reshape(seq_dev * res_dev, width)
    query = (jnp.dot(flat, w_query, preferred_element_type=jnp.float32) * scale).astype(
        jnp.bfloat16
    )
    query = query.reshape(seq_dev, res_dev, heads, head_dim)
    keyval = jnp.dot(flat, w_keyval, preferred_element_type=jnp.float32).astype(jnp.bfloat16)
    keys = keyval[:, :width].reshape(seq_dev, res_dev, width)
    values = keyval[:, width:].reshape(seq_dev, res_dev, width)
    piece = lax.all_gather(keys, "res", axis=1, tiled=True)
    block = piece.reshape(piece.shape[0], piece.shape[1], heads, head_dim)
    partial_logits = jnp.einsum("sihd,sjhd->hij", query, block, preferred_element_type=jnp.float32)
    probs = softmax_rows(lax.psum(partial_logits, "seq"))
    piece = lax.all_gather(values, "res", axis=1, tiled=True)
    block = piece.reshape(piece.shape[0], piece.shape[1], heads, head_dim)
    attended = jnp.einsum("hij,sjhd->sihd", probs, block, preferred_element_type=jnp.float32)
    attended = attended.astype(jnp.bfloat16).reshape(seq_dev * res_dev, width)
    mixed = jnp.dot(attended, w_out, preferred_element_type=jnp.float32)
    return mixed.reshape(seq_dev, res_dev, width)


def solution(mesh):
    return jax.shard_map(
        local,
        mesh=mesh,
        in_specs=(P("seq", "res", None), P(), P(), P()),
        out_specs=P("seq", "res", None),
        check_vma=False,
    )
```

profile of v0, /device:TPU:0, one launch (start us, length us, event | category | flops | bytes accessed | tf_op | source)
XLA Modules:
  0.0 402.9 jit_solution(13123193494965191811)
XLA Ops:
  6.5 0.0 copy-start
  6.5 0.0 all-gather.5.cloned.1.call-start
  6.5 1.7 copy-done
  8.2 3.3 convolution_convert_fusion
  11.5 1.6 fusion.16
  13.0 0.0 copy-start.2
  13.0 0.0 copy-start.3
  13.0 0.0 all-gather.5.cloned.1.call-update
  13.1 0.0 all-gather.3.cloned.1.call-start
  13.1 0.7 all-gather.3.cloned.1.call-update
  13.8 0.0 all-reduce.2.cloned.1.call-start
  13.9 0.4 copy-done.2
  14.3 0.4 copy-done.3
  14.7 1.1 multiply_convert_fusion
  15.7 3.3 reshape.27
  19.0 98.1 %all-gather.5.cloned.1.call-done = bf16[12,1024,768]{2,1,0:T(8,128)(2,1)} async-done(((bf16[12,64,768]{2,1,0:T(8,128)(2,1)}), bf16[12,1024,768]{2,1,0:T(8,128)(2,1)}) %all-gather.5.cloned.1.call-update) | async-done | bytes 18874384 | tf_op jit(solution)/shard_map/all_gather | solution.py:30
  117.2 24.7 %copy.13 = bf16[12,1024,768]{1,2,0:T(8,128)(2,1)} copy(bf16[12,1024,768]{2,1,0:T(8,128)(2,1)} %all-gather.5.cloned.1.call-done) | data formatting | bytes 37748736 | tf_op jit(solution)/shard_map/all_gather | solution.py:30
  141.9 12.8 %fusion.8 = f32[12,64,1024]{2,1,0:T(8,128)} fusion(bf16[12,1024,12,64]{1,3,2,0:T(8,128)(2,1)} %bitcast.25, bf16[12,64,12,64]{3,2,1,0:T(8,128)(2,1)} %reshape.27), kind=kOutput, calls=%fused_computation.11 | convolution fusion | flops 1207959552 | bytes 23199744 | tf_op jit(solution)/shard_map/sihd,sjhd->hij/dot_general | solution.py:32
  154.7 0.0 all-reduce.2.cloned.1.call-update
  154.7 66.4 %all-gather.3.cloned.1.call-done = bf16[12,1024,768]{2,1,0:T(8,128)(2,1)} async-done(((bf16[12,64,768]{2,1,0:T(8,128)(2,1)}), bf16[12,1024,768]{2,1,0:T(8,128)(2,1)}) %all-gather.3.cloned.1.call-update) | async-done | bytes 18874384 | tf_op jit(solution)/shard_map/all_gather | solution.py:34
  221.1 24.4 %copy.12 = bf16[12,1024,768]{1,2,0:T(8,128)(2,1)} copy(bf16[12,1024,768]{2,1,0:T(8,128)(2,1)} %all-gather.3.cloned.1.call-done) | data formatting | bytes 37748736 | tf_op jit(solution)/shard_map/all_gather | solution.py:34
  245.6 126.9 %all-reduce.2.cloned.1.call-done = f32[12,64,1024]{2,1,0:T(8,128)} async-done(((f32[12,64,1024]{2,1,0:T(8,128)}), f32[12,64,1024]{2,1,0:T(8,128)}) %all-reduce.2.cloned.1.call-update) | async-done | bytes 3145744 | tf_op jit(solution)/shard_map/psum | solution.py:33
  372.4 3.5 fusion.17
  375.9 9.1 %convert_bitcast_fusion = bf16[12,64,12,64]{1,3,0,2:T(8,128)(2,1)S(1)} fusion(bf16[12,1024,12,64]{1,3,2,0:T(8,128)(2,1)} %bitcast.24, f32[12,64,1024]{2,1,0:T(8,128)S(1)} %get-tuple-element.8, f32[12,64]{1,0:T(8,128)S(1)} %get-tuple-element.7), kind=kOutput, calls=%fused_computation.9 | convolution fusion | flops 1210122240 | bytes 23202816 | tf_op jit(solution)/shard_map/hij,sjhd->sihd/dot_general | solution.py:36
  385.0 3.6 copy.17
  388.6 0.0 copy-start.1
  388.6 4.0 dot_general.21
  392.6 3.8 fusion.14
  396.4 0.0 copy-done.1
Async XLA Ops:
  6.5 1.7 copy-start
  6.5 110.6 %all-gather.5.cloned.1.call-start = ((), (), s32[]{:S(2)}) async-start(), calls=%async_computation.1 | async-start | bytes 20054016 | tf_op jit(solution)/shard_map/all_gather | solution.py:30
  13.0 1.3 copy-start.2
  13.0 1.6 copy-start.3
  13.1 208.1 %all-gather.3.cloned.1.call-start = ((), (), s32[]{:S(2)}) async-start(), calls=%async_computation | async-start | bytes 20054016 | tf_op jit(solution)/shard_map/all_gather | solution.py:34
  13.8 358.6 %all-reduce.2.cloned.1.call-start = ((), (), s32[]{:S(2)}) async-start(), calls=%async_computation.2 | async-start | bytes 6291456 | tf_op jit(solution)/shard_map/psum | solution.py:33
  388.6 7.8 %copy-start.1 = (bf16[768,1536]{1,0:T(8,128)(2,1)S(1)}, bf16[768,1536]{1,0:T(8,128)(2,1)}, u32[]{:S(2)}) copy-start(bf16[768,1536]{1,0:T(8,128)(2,1)} %param.6) | copy-start | bytes 7077892
Sparse Core Ops, SparseCore 0:
  13.2 103.9 all-gather.4
  118.8 102.2 all-gather.2
  223.6 148.7 all-reduce.1
where the time goes:
time: 406 us; the launch traced here: 403 us
  waiting for transfers between devices  292 us (72%)
  local copies, waits for them, and re-layouts  64.1 us (16%)
  matrix products  30 us (7%)
  between operations  13.1 us (3%)
    psum x1, waiting for transfers between devices, local(): probs = softmax_rows(lax.psum(partial_logits, 'seq'))  127 us
    all_gather x1, waiting for transfers between devices, local(): piece = lax.all_gather(keys, 'res', axis=1, tiled=True)  98.1 us
    all_gather x1, waiting for transfers between devices, local(): piece = lax.all_gather(values, 'res', axis=1, tiled=True)  66.4 us
    all_gather x1, local copies, waits for them, and re-layouts, local(): piece = lax.all_gather(keys, 'res', axis=1, tiled=True)  24.7 us
    all_gather x1, local copies, waits for them, and re-layouts, local(): piece = lax.all_gather(values, 'res', axis=1, tiled=True)  24.4 us
    dot_general x1, matrix products, local(): jnp.einsum('sihd,sjhd->hij', query, block, preferred_element_type=jnp.flo...  12.8 us
    dot_general x1, matrix products, local(): jnp.einsum('hij,sjhd->sihd', probs, block, preferred_element_type=jnp.flo...  9.08 us
  transfers between devices with their start and end apart: 3, of which 3 were waited for; matrix products, arithmetic and copies ran while one was open for 16% of the time, Pallas kernels for 0%

commit v1 on v0

v1 whole, which is shorter than its diff:
```python
import functools
import math

import jax
import jax.numpy as jnp
from jax import lax
from jax.experimental import pallas as pl
from jax.experimental.pallas import tpu as pltpu
from jax.sharding import PartitionSpec as P

DH = 64
NX, NY = 4, 4
MESH = pl.DeviceIdType.MESH
BF16, F32 = jnp.bfloat16, jnp.float32


def layer_kernel(
    scale,
    tok_hbm, wq_hbm, wkv_hbm, out_ref,
    tok, wq, wkv, q_mine, k_mine, v_mine, q_all, k_all, v_all,
    scores, part_out, part_in, own_rows, pair_out, pair_in, probs, att_out, att_all,
    load_sem, send_sem, recv_sem,
):
    seq, res = lax.axis_index("seq"), lax.axis_index("res")
    y, zh = lax.div(seq, 2), lax.rem(seq, 2)
    zl, x, c = lax.div(res, 8), lax.rem(lax.div(res, 2), NX), lax.rem(res, 2)
    width = tok.shape[1]
    heads = q_mine.shape[0]
    per = heads // NX
    cols = 256

    def at_x(k):
        return (seq, zl * 8 + lax.rem(x + k, NX) * 2 + c)

    def at_y(k):
        return (lax.rem(y + k, NY) * 2 + zh, res)

    at_zl = (seq, (1 - zl) * 8 + x * 2 + c)
    at_core = (seq, zl * 8 + x * 2 + (1 - c))
    at_zh = (y * 2 + (1 - zh), res)

    copies = {}

    def send(kind, slot, hh, k, src, dst, where):
        copy = pltpu.make_async_remote_copy(
            src_ref=src, dst_ref=dst,
            send_sem=send_sem.at[slot, hh, k], recv_sem=recv_sem.at[slot, hh, k],
            device_id=where, device_id_type=MESH,
        )
        copy.start()
        copies[kind, hh, k] = copy

    def arrived(kind, hh, k):
        copies[kind, hh, k].wait_recv()

    half = wkv.shape[1] // 2
    loads = [
        pltpu.make_async_copy(tok_hbm, tok, load_sem.at[0]),
        pltpu.make_async_copy(wkv_hbm.at[:, pl.ds(0, half)], wkv.at[:, pl.ds(0, half)], load_sem.at[1]),
        pltpu.make_async_copy(wq_hbm, wq, load_sem.at[2]),
        pltpu.make_async_copy(wkv_hbm.at[:, pl.ds(half, half)], wkv.at[:, pl.ds(half, half)], load_sem.at[3]),
    ]
    for load in loads:
        load.start()

    barrier = pltpu.get_barrier_semaphore()
    others = [at_x(1), at_x(2), at_x(3), at_y(1), at_y(2), at_y(3), at_zl, at_core, at_zh]
    for other in others:
        pl.semaphore_signal(barrier, inc=1, device_id=other, device_id_type=MESH)

    def low_lanes(rows):
        return lax.broadcasted_iota(jnp.int32, (rows, 128), 1) < DH

    def project(w, first, dst, factor):
        low = low_lanes(64)

        @pl.loop(0, width // cols)
        def _(n):
            at = pl.multiple_of(first + n * cols, cols)
            acc = jnp.dot(tok[...], w[:, pl.ds(at, cols)], preferred_element_type=F32)
            if factor is not None:
                acc = acc * factor
            for pair in range(cols // 128):
                for m in range(tok.shape[0] // 128):
                    even = acc[m * 128:m * 128 + 64, pair * 128:pair * 128 + 128]
                    odd = pltpu.roll(acc[m * 128 + 64:m * 128 + 128, pair * 128:pair * 128 + 128], 64, 1)
                    head = n * (cols // DH) + 2 * pair
                    dst[head, :, m * 128:m * 128 + 128] = jnp.where(low, even, odd).astype(BF16)
                    dst[head + 1, :, m * 128:m * 128 + 128] = jnp.where(low, odd, even).astype(BF16)

    mine = c * 2 + zl
    theirs = c * 2 + (1 - zl)

    def kv_send(kind, slot, src, dst, hh):
        dst[hh, mine, x] = src[per * x + hh]
        for k in (1, 3, 2):
            to = lax.rem(x + k, NX)
            send(kind + "x", slot, hh, k, src.at[per * to + hh], dst.at[hh, mine, x], at_x(k))

    def kv_own(kind, slot, src, dst, hh):
        send(kind + "z", slot + 1, hh, 0, src.at[per * x + hh], dst.at[hh, mine, x], at_zl)

    def kv_forward(kind, slot, dst, hh):
        for k in (1, 3, 2):
            arrived(kind + "x", hh, k)
            block = dst.at[hh, mine, lax.rem(x + NX - k, NX)]
            send(kind + "z", slot + 1, hh, k, block, block, at_zl)
        send(kind + "c", slot + 2, hh, 0, dst.at[hh, mine], dst.at[hh, mine], at_core)

    def kv_last(kind, slot, dst, hh):
        for k in (0, 1, 3, 2):
            arrived(kind + "z", hh, k)
        send(kind + "c", slot + 2, hh, 1, dst.at[hh, theirs], dst.at[hh, theirs], at_core)
        arrived(kind + "c", hh, 0)
        arrived(kind + "c", hh, 1)

    def q_send(hh):
        q_all[hh, x] = q_mine[per * x + hh]
        for k in (2, 1, 3):
            to = lax.rem(x + k, NX)
            send("q", 6, hh, k, q_mine.at[per * to + hh], q_all.at[hh, x], at_x(k))

    def logits(hh):
        for k in (2, 1, 3):
            arrived("q", hh, k)

        @pl.loop(0, 4)
        def _(t):
            s = lax.dot_general(
                q_all[hh].reshape(256, width), k_all[hh, t].reshape(256, width),
                (((1,), (1,)), ((), ())), preferred_element_type=F32,
            ).reshape(NX, 64, 256)
            at = pl.ds(pl.multiple_of(t * 256, 256), 256)
            scores[:, :, at] = s
            part_out[hh, :, :, at] = s.astype(BF16)

        own_rows[hh] = scores[y]
        for k in (2, 1, 3):
            send("r", 7, hh, k, part_out.at[hh, lax.rem(y + k, NY)], part_in.at[hh, k - 1], at_y(k))

    def add_rows(hh):
        for k in (2, 1, 3):
            arrived("r", hh, k)
        total = own_rows[hh]
        for k in range(3):
            total = total + part_in[hh, k].astype(F32)
        own_rows[hh] = total
        pair_out[hh] = total.astype(BF16)
        send("p", 8, hh, 0, pair_out.at[hh], pair_in.at[hh], at_zh)

    def softmax(hh):
        arrived("p", hh, 0)
        rows = own_rows[hh] + pair_in[hh].astype(F32)
        weights = jnp.exp(rows - jnp.max(rows, axis=-1, keepdims=True))
        probs[hh, y] = (weights / jnp.sum(weights, axis=-1, keepdims=True)).astype(BF16)
        for k in (2, 1, 3):
            send("a", 9, hh, k, probs.at[hh, y], probs.at[hh, y], at_y(k))

    def attend(hh):
        for k in (2, 1, 3):
            arrived("a", hh, k)

        @pl.loop(0, width // cols)
        def _(n):
            at = pl.ds(pl.multiple_of(n * cols, cols), cols)
            o = jnp.dot(
                probs[hh].reshape(256, 1024), v_all[hh, :, :, :, at].reshape(1024, cols),
                preferred_element_type=F32,
            )
            att_out[hh, :, :, at] = o.astype(BF16).reshape(NX, 64, cols)

        att_all[per * x + hh] = att_out[hh, x]
        for k in (2, 1, 3):
            to = lax.rem(x + k, NX)
            send("o", 10, hh, k, att_out.at[hh, to], att_all.at[per * x + hh], at_x(k))

    loads[0].wait()
    loads[1].wait()
    project(wkv, 0, k_mine, None)
    pl.semaphore_wait(barrier, len(others))
    kv_send("k", 0, k_mine, k_all, 0)
    kv_own("k", 0, k_mine, k_all, 0)
    loads[2].wait()
    project(wq, 0, q_mine, scale)
    q_send(0)
    for hh in range(1, per):
        kv_send("k", 0, k_mine, k_all, hh)
        q_send(hh)
    loads[3].wait()
    project(wkv, half, v_mine, None)
    for hh in range(per):
        kv_send("v", 3, v_mine, v_all, hh)

    kv_forward("k", 0, k_all, 0)
    kv_own("k", 0, k_mine, k_all, 1)
    kv_last("k", 0, k_all, 0)
    logits(0)
    kv_forward("k", 0, k_all, 1)
    kv_own("k", 0, k_mine, k_all, 2)
    add_rows(0)
    kv_last("k", 0, k_all, 1)
    logits(1)
    kv_forward("k", 0, k_all, 2)
    softmax(0)
    kv_own("v", 3, v_mine, v_all, 0)
    add_rows(1)
    kv_last("k", 0, k_all, 2)
    logits(2)
    kv_forward("v", 3, v_all, 0)
    softmax(1)
    kv_own("v", 3, v_mine, v_all, 1)
    add_rows(2)
    kv_last("v", 3, v_all, 0)
    attend(0)
    kv_forward("v", 3, v_all, 1)
    softmax(2)
    kv_own("v", 3, v_mine, v_all, 2)
    kv_forward("v", 3, v_all, 2)
    kv_last("v", 3, v_all, 1)
    attend(1)
    kv_last("v", 3, v_all, 2)
    attend(2)

    for hh in range(per):
        for k in (2, 1, 3):
            arrived("o", hh, k)
    low = low_lanes(64)
    for pair in range(heads // 2):
        at = pl.ds(pair * 128, 128)
        for m in range(width // 128):
            a = att_all[2 * pair, :, m * 128:m * 128 + 128].astype(F32)
            b = att_all[2 * pair + 1, :, m * 128:m * 128 + 128].astype(F32)
            out_ref[m * 128:m * 128 + 64, at] = jnp.where(low, a, b).astype(BF16)
            out_ref[m * 128 + 64:m * 128 + 128, at] = pltpu.roll(jnp.where(low, b, a), 64, 1).astype(BF16)
    for copy in copies.values():
        copy.wait_send()


def local(tokens, w_query, w_keyval, w_out):
    seq_dev, res_dev, width = tokens.shape
    heads = width // DH
    per = heads // NX
    scale = 1.0 / math.sqrt(DH * seq_dev * lax.axis_size("seq"))
    flat = tokens.reshape(seq_dev * res_dev, width)
    rows = seq_dev * res_dev
    any_spec = pl.BlockSpec(memory_space=pl.ANY)
    block = (heads, res_dev, seq_dev * DH)
    attended = pl.pallas_call(
        functools.partial(layer_kernel, scale),
        out_shape=jax.ShapeDtypeStruct((rows, width), BF16),
        in_specs=[any_spec] * 3,
        out_specs=pl.BlockSpec(memory_space=pltpu.VMEM),
        scratch_shapes=[
            pltpu.VMEM((rows, width), BF16),
            pltpu.VMEM((width, width), BF16),
            pltpu.VMEM((width, 2 * width), BF16),
            pltpu.VMEM(block, BF16),
            pltpu.VMEM(block, BF16),
            pltpu.VMEM(block, BF16),
            pltpu.VMEM((per, NX, res_dev, seq_dev * DH), BF16),
            pltpu.VMEM((per, 4, NX, res_dev, seq_dev * DH), BF16),
            pltpu.VMEM((per, 4, NX, res_dev, seq_dev * DH), BF16),
            pltpu.VMEM((NX, res_dev, 1024), F32),
            pltpu.VMEM((per, NY, res_dev, 1024), BF16),
            pltpu.VMEM((per, 3, res_dev, 1024), BF16),
            pltpu.VMEM((per, res_dev, 1024), F32),
            pltpu.VMEM((per, res_dev, 1024), BF16),
            pltpu.VMEM((per, res_dev, 1024), BF16),
            pltpu.VMEM((per, NY, res_dev, 1024), BF16),
            pltpu.VMEM((per, NX, res_dev, seq_dev * DH), BF16),
            pltpu.VMEM(block, BF16),
            pltpu.SemaphoreType.DMA((4,)),
            pltpu.SemaphoreType.DMA((11, per, 4)),
            pltpu.SemaphoreType.DMA((11, per, 4)),
        ],
        cost_estimate=pl.CostEstimate(flops=5 * 10**9, bytes_accessed=10**7, transcendentals=2 * 10**5),
        compiler_params=pltpu.CompilerParams(
            collective_id=0, has_side_effects=True, vmem_limit_bytes=56 * 2**20
        ),
        name="tied_row_attention",
    )(flat, w_query, w_keyval)
    mixed = jnp.dot(attended, w_out, preferred_element_type=F32)
    return mixed.reshape(seq_dev, res_dev, width)


def solution(mesh):
    return jax.shard_map(
        local,
        mesh=mesh,
        in_specs=(P("seq", "res", None), P(), P(), P()),
        out_specs=P("seq", "res", None),
        check_vma=False,
    )
```

time: 406 us -> 91.6 us (0.23)
  waiting for transfers between devices: 292 us -> 0 us
  Pallas kernels: 0 us -> 86.8 us
  local copies, waits for them, and re-layouts: 64.1 us -> 0.01 us
  matrix products: 30 us -> 3.76 us
  between operations: 13.1 us -> 0.02 us
    all_gather x2 -> x0, waiting for transfers between devices: 165 us -> none  [the longest x1 98.1 us: local(): piece = lax.all_gather(keys, 'res', axis=1, tiled=True)]
    psum x1 -> x0, waiting for transfers between devices: 127 us -> none  [local(): probs = softmax_rows(lax.psum(partial_logits, 'seq'))]
    pallas_call x0 -> x1, Pallas kernels: none -> 86.8 us  [local(): pl.pallas_call(functools.partial(layer_kernel, scale), out_shape=jax.Shap...]
    all_gather x2 -> x0, local copies, waits for them, and re-layouts: 49.1 us -> none  [the longest x1 24.7 us: local(): piece = lax.all_gather(keys, 'res', axis=1, tiled=True)]
    dot_general x5 -> x1, matrix products: 30 us -> 3.76 us  [local(): mixed = jnp.dot(attended, w_out, preferred_element_type=F32)]
  transfers between devices with their start and end apart: 3 -> 0, of which waited for: 3 -> 0; matrix products, arithmetic and copies ran while one was open for 16% -> 0% of each run, Pallas kernels for 0% -> 0%
where the time goes in v1:
time: 91.6 us; the launch traced here: 90.5 us
  Pallas kernels  86.8 us (95%)
  matrix products  3.76 us (4%)
    pallas_call x1, Pallas kernels, local(): pl.pallas_call(functools.partial(layer_kernel, scale), out_shape=jax.Shap...  86.8 us
    dot_general x1, matrix products, local(): mixed = jnp.dot(attended, w_out, preferred_element_type=F32)  3.76 us

profile of v1, /device:TPU:0, one launch (start us, length us, event | category | flops | bytes accessed | tf_op | source)
XLA Modules:
  0.0 90.5 jit_solution(13719302993169755376)
XLA Ops:
  0.0 0.0 copy-start
  0.0 86.8 %tied_row_attention.1 = bf16[768,768]{1,0:T(8,128)(2,1)} custom-call(bf16[768,768]{1,0:T(8,128)(2,1)} %bitcast.4, bf16[768,768]{1,0:T(8,128)(2,1)} %wq_hbm.1, bf16[768,1536]{1,0:T(8,128)(2,1)} %wkv_hbm.1), custom_call_target="tpu_custom_call" | custom-call | flops 5000000000 | bytes 10000000 | tf_op jit(solution)/shard_map/tied_row_attention/pallas_call | solution.py:248
  86.8 0.0 copy-done
  86.8 3.8 %fusion = f32[768,768]{1,0:T(8,128)} fusion(bf16[768,768]{1,0:T(8,128)(2,1)} %tied_row_attention.1, bf16[768,768]{1,0:T(8,128)(2,1)S(1)} %copy-done), kind=kOutput, calls=%fused_computation | convolution fusion | flops 905969664 | bytes 4718592 | tf_op jit(solution)/shard_map/dot_general | solution.py:282
Async XLA Ops:
  0.0 86.8 %copy-start = (bf16[768,768]{1,0:T(8,128)(2,1)S(1)}, bf16[768,768]{1,0:T(8,128)(2,1)}, u32[]{:S(2)}) copy-start(bf16[768,768]{1,0:T(8,128)(2,1)} %param.7) | copy-start | bytes 3538948

commit v2 on v1

v2 whole, which is shorter than its diff:
```python
import functools
import math

import jax
import jax.numpy as jnp
from jax import lax
from jax.experimental import pallas as pl
from jax.experimental.pallas import tpu as pltpu
from jax.sharding import PartitionSpec as P

DH = 64
NX, NY = 4, 4
COLS = 256
MORE = 128
MESH = pl.DeviceIdType.MESH
BF16, F32 = jnp.bfloat16, jnp.float32


def layer_kernel(
    scale,
    tok_hbm, wq_hbm, wkv_hbm, wout_hbm, out_hbm,
    tok, wq, wkv, wout, q_mine, k_mine, v_mine, k_more, v_more, q_all, k_all, v_all,
    scores, part_out, part_in, own_rows, pair_out, pair_in, probs, att_out, att_all, left, mixed,
    load_sem, send_sem, recv_sem,
):
    seq, res = lax.axis_index("seq"), lax.axis_index("res")
    y, zh = lax.div(seq, 2), lax.rem(seq, 2)
    zl, x, c = lax.div(res, 8), lax.rem(lax.div(res, 2), NX), lax.rem(res, 2)
    rows, width = tok_hbm.shape
    heads = q_mine.shape[0]
    per = heads // NX

    def at_x(k):
        return (seq, zl * 8 + lax.rem(x + k, NX) * 2 + c)

    def at_y(k):
        return (lax.rem(y + k, NY) * 2 + zh, res)

    at_zl = (seq, (1 - zl) * 8 + x * 2 + c)
    at_core = (seq, zl * 8 + x * 2 + (1 - c))
    at_zh = (y * 2 + (1 - zh), res)

    copies = {}
    seen = set()
    slots = ["kx", "kz", "kc", "kt", "vx", "vz", "vc", "vt", "q", "r", "p", "a", "o", "t"]

    def send(kind, stage, k, src, dst, where):
        slot = slots.index(kind)
        copy = pltpu.make_async_remote_copy(
            src_ref=src, dst_ref=dst,
            send_sem=send_sem.at[slot, stage, k], recv_sem=recv_sem.at[slot, stage, k],
            device_id=where, device_id_type=MESH,
        )
        copy.start()
        copies[kind, stage, k] = copy

    def arrived(kind, stage, *ks):
        for k in ks:
            if (kind, stage, k) not in seen:
                seen.add((kind, stage, k))
                copies[kind, stage, k].wait_recv()

    half = wkv.shape[1] // 2
    loads = [
        pltpu.make_async_copy(tok_hbm.at[pl.ds(0, 128)], tok.at[pl.ds(0, 128)], load_sem.at[0]),
        pltpu.make_async_copy(tok_hbm.at[pl.ds(128, rows - 128)], tok.at[pl.ds(128, rows - 128)], load_sem.at[1]),
        pltpu.make_async_copy(wkv_hbm.at[:, pl.ds(0, half)], wkv.at[:, pl.ds(0, half)], load_sem.at[2]),
        pltpu.make_async_copy(wq_hbm, wq, load_sem.at[3]),
        pltpu.make_async_copy(wkv_hbm.at[:, pl.ds(half, half)], wkv.at[:, pl.ds(half, half)], load_sem.at[4]),
    ] + [pltpu.make_async_copy(wout_hbm.at[:, hh], wout.at[hh], load_sem.at[5 + hh]) for hh in range(per)]
    for load in loads[:3]:
        load.start()

    barrier = pltpu.get_barrier_semaphore()
    others = [at_x(1), at_x(2), at_x(3), at_y(1), at_y(2), at_y(3), at_zl, at_core, at_zh]
    for other in others:
        pl.semaphore_signal(barrier, inc=1, device_id=other, device_id_type=MESH)
    for load in loads[3:]:
        load.start()

    low = lax.broadcasted_iota(jnp.int32, (64, 128), 1) < DH

    def project(w, first, dst, factor=None, row=0, pairs=rows // 128):
        @pl.loop(0, width // COLS)
        def _(n):
            at = pl.multiple_of(first + n * COLS, COLS)
            acc = jnp.dot(tok[row:row + pairs * 128], w[:, pl.ds(at, COLS)], preferred_element_type=F32)
            if factor is not None:
                acc = acc * factor
            for pair in range(COLS // 128):
                for m in range(pairs):
                    even = acc[m * 128:m * 128 + 64, pair * 128:pair * 128 + 128]
                    odd = pltpu.roll(acc[m * 128 + 64:m * 128 + 128, pair * 128:pair * 128 + 128], 64, 1)
                    head = n * (COLS // DH) + 2 * pair
                    dst[head, :, m * 128:m * 128 + 128] = jnp.where(low, even, odd).astype(BF16)
                    dst[head + 1, :, m * 128:m * 128 + 128] = jnp.where(low, odd, even).astype(BF16)

    mine = c * 2 + zl
    theirs = c * 2 + (1 - zl)
    kv = {"k": (k_mine, k_all, k_more), "v": (v_mine, v_all, v_more)}

    def columns(stage):
        return {2: (2, 0, width), 3: (2, 0, 512), 4: (2, 512, 256)}.get(stage, (stage, 0, width))

    def kv_send(kind, hh):
        src, dst, _ = kv[kind]
        dst[hh, mine, x] = src[per * x + hh]
        for k in (1, 3, 2):
            to = lax.rem(x + k, NX)
            send(kind + "x", hh, k, src.at[per * to + hh], dst.at[hh, mine, x], at_x(k))

    def kv_more(kind):
        arrived("t", 0, 0)
        _, dst, src = kv[kind]
        project(wkv, 0 if kind == "k" else half, src, row=rows, pairs=1)
        for hh in range(per):
            dst[hh, theirs, x, :, 0:MORE] = src[per * x + hh]
        for k in (2, 1, 3):
            to = lax.rem(x + k, NX)
            send(
                kind + "t", 0, k, src.at[pl.ds(per * to, per)],
                dst.at[pl.ds(0, per), theirs, x, :, pl.ds(0, MORE)], at_x(k),
            )

    def across(stage):
        hh, lo, n = columns(stage)
        first = max(lo, MORE)
        return hh, pl.ds(first, lo + n - first)

    def kv_own(kind, stage):
        src, dst, _ = kv[kind]
        hh, at = across(stage)
        send(kind + "z", stage, 0, src.at[per * x + hh, :, at], dst.at[hh, mine, x, :, at], at_zl)

    def kv_forward(kind, stage):
        _, dst, _ = kv[kind]
        hh, at = across(stage)
        for k in (1, 3, 2):
            arrived(kind + "x", hh, k)
            block = dst.at[hh, mine, lax.rem(x + NX - k, NX), :, at]
            send(kind + "z", stage, k, block, block, at_zl)
        hh, lo, n = columns(stage)
        blocks = dst.at[hh, mine, :, :, pl.ds(lo, n)]
        send(kind + "c", stage, 0, blocks, blocks, at_core)

    def kv_last(kind, stage):
        _, dst, _ = kv[kind]
        arrived(kind + "t", 0, 2, 1, 3)
        arrived(kind + "z", stage, 0, 1, 3, 2)
        hh, lo, n = columns(stage)
        blocks = dst.at[hh, theirs, :, :, pl.ds(lo, n)]
        send(kind + "c", stage, 1, blocks, blocks, at_core)
        arrived(kind + "c", stage, 0, 1)

    def q_send(hh):
        q_all[hh, x] = q_mine[per * x + hh]
        for k in (2, 1, 3):
            to = lax.rem(x + k, NX)
            send("q", hh, k, q_mine.at[per * to + hh], q_all.at[hh, x], at_x(k))

    def logits(hh):
        arrived("q", hh, 2, 1, 3)

        @pl.loop(0, 4)
        def _(t):
            s = lax.dot_general(
                q_all[hh].reshape(256, width), k_all[hh, t].reshape(256, width),
                (((1,), (1,)), ((), ())), preferred_element_type=F32,
            ).reshape(NX, 64, 256)
            at = pl.ds(pl.multiple_of(t * 256, 256), 256)
            scores[:, :, at] = s
            part_out[hh, :, :, at] = s.astype(BF16)

        own_rows[hh] = scores[y]
        for k in (2, 1, 3):
            send("r", hh, k, part_out.at[hh, lax.rem(y + k, NY)], part_in.at[hh, k - 1], at_y(k))

    def add_rows(hh):
        arrived("r", hh, 2, 1, 3)
        total = own_rows[hh]
        for k in range(3):
            total = total + part_in[hh, k].astype(F32)
        own_rows[hh] = total
        pair_out[hh] = total.astype(BF16)
        send("p", hh, 0, pair_out.at[hh], pair_in.at[hh], at_zh)

    def softmax(hh):
        arrived("p", hh, 0)
        total = own_rows[hh] + pair_in[hh].astype(F32)
        weights = jnp.exp(total - jnp.max(total, axis=-1, keepdims=True))
        probs[hh, y] = (weights / jnp.sum(weights, axis=-1, keepdims=True)).astype(BF16)
        for k in (2, 1, 3):
            send("a", hh, k, probs.at[hh, y], probs.at[hh, y], at_y(k))

    def attend(stage):
        hh, lo, n = columns(stage)
        arrived("a", hh, 2, 1, 3)

        @pl.loop(lo // COLS, (lo + n) // COLS)
        def _(tile):
            at = pl.ds(pl.multiple_of(tile * COLS, COLS), COLS)
            o = jnp.dot(
                probs[hh].reshape(256, 1024), v_all[hh, :, :, :, at].reshape(1024, COLS),
                preferred_element_type=F32,
            )
            att_out[hh, :, :, at] = o.astype(BF16).reshape(NX, 64, COLS)

        at = pl.ds(lo, n)
        att_all[per * x + hh, :, at] = att_out[hh, x, :, at]
        for k in (2, 1, 3):
            to = lax.rem(x + k, NX)
            send("o", stage, k, att_out.at[hh, to, :, at], att_all.at[per * x + hh, :, at], at_x(k))

    def project_out(stage):
        hh, lo, n = columns(stage)
        arrived("o", stage, 2, 1, 3)
        if stage == 0:
            for load in loads[5:]:
                load.wait()
        for m in range(lo // 128, (lo + n) // 128):
            for pair in range(NX // 2):
                a = att_all[2 * pair * per + hh, :, m * 128:m * 128 + 128].astype(F32)
                b = att_all[(2 * pair + 1) * per + hh, :, m * 128:m * 128 + 128].astype(F32)
                halves = [jnp.where(low, a, b), pltpu.roll(jnp.where(low, b, a), 64, 1)]
                for s in range(2):
                    left[m * 128 + s * 64:m * 128 + s * 64 + 64, pair * 128:pair * 128 + 128] = halves[
                        (s + hh) % 2
                    ].astype(BF16)
        part = pl.ds(lo, n)

        @pl.loop(0, width // COLS)
        def _(tile):
            at = pl.ds(pl.multiple_of(tile * COLS, COLS), COLS)
            o = jnp.dot(left[part, :], wout[hh, :, :, at].reshape(NX * DH, COLS), preferred_element_type=F32)
            mixed[part, at] = o if hh == 0 else mixed[part, at] + o

    def store(stage):
        _, lo, n = columns(stage)
        copy = pltpu.make_async_copy(mixed.at[pl.ds(lo, n)], out_hbm.at[pl.ds(lo, n)], load_sem.at[5 + stage])
        copy.start()
        return copy

    def start_tokens():
        loads[0].wait()
        pl.semaphore_wait(barrier, len(others))
        send("t", 0, 0, tok.at[pl.ds(0, 128)], tok.at[pl.ds(rows, 128)], at_zl)

    def project_keys():
        loads[1].wait()
        loads[2].wait()
        project(wkv, 0, k_mine)

    def project_query():
        loads[3].wait()
        project(wq, 0, q_mine, scale)

    def project_values():
        loads[4].wait()
        project(wkv, half, v_mine)

    start_tokens()
    project_keys()
    kv_send("k", 0)
    kv_own("k", 0)
    kv_own("k", 1)
    project_query()
    kv_send("k", 1)
    kv_more("k")
    kv_forward("k", 0)
    q_send(0)
    kv_send("k", 2)
    q_send(1)
    kv_own("k", 2)
    project_values()
    q_send(2)
    kv_forward("k", 1)
    kv_send("v", 0)
    kv_send("v", 1)
    kv_own("v", 4)
    kv_last("k", 0)
    logits(0)
    kv_send("v", 2)
    kv_forward("k", 2)
    kv_more("v")
    kv_last("k", 1)
    kv_own("v", 0)
    logits(1)
    add_rows(0)
    kv_last("k", 2)
    kv_own("v", 1)
    logits(2)
    kv_forward("v", 0)
    softmax(0)
    add_rows(1)
    add_rows(2)
    kv_forward("v", 1)
    kv_forward("v", 3)
    softmax(1)
    kv_last("v", 0)
    kv_own("v", 3)
    softmax(2)
    kv_forward("v", 4)
    attend(0)
    kv_last("v", 1)
    attend(1)
    kv_last("v", 3)
    attend(3)
    kv_last("v", 4)
    attend(4)
    project_out(0)
    project_out(1)
    project_out(3)
    project_out(4)

    stores = [store(3), store(4)]
    for copy in copies.values():
        copy.wait_send()
    for copy in stores:
        copy.wait()


def local(tokens, w_query, w_keyval, w_out):
    seq_dev, res_dev, width = tokens.shape
    heads = width // DH
    per = heads // NX
    scale = 1.0 / math.sqrt(DH * seq_dev * lax.axis_size("seq"))
    rows = seq_dev * res_dev
    block = (heads, res_dev, seq_dev * DH)
    mixed = pl.pallas_call(
        functools.partial(layer_kernel, scale),
        out_shape=jax.ShapeDtypeStruct((rows, width), F32),
        in_specs=[pl.BlockSpec(memory_space=pltpu.HBM)] * 4,
        out_specs=pl.BlockSpec(memory_space=pl.ANY),
        scratch_shapes=[
            pltpu.VMEM((rows + 128, width), BF16),
            pltpu.VMEM((width, width), BF16),
            pltpu.VMEM((width, 2 * width), BF16),
            pltpu.VMEM((per, NX, DH, width), BF16),
            pltpu.VMEM(block, BF16),
            pltpu.VMEM(block, BF16),
            pltpu.VMEM(block, BF16),
            pltpu.VMEM((heads, res_dev, MORE), BF16),
            pltpu.VMEM((heads, res_dev, MORE), BF16),
            pltpu.VMEM((per, NX, res_dev, seq_dev * DH), BF16),
            pltpu.VMEM((per, 4, NX, res_dev, seq_dev * DH), BF16),
            pltpu.VMEM((per, 4, NX, res_dev, seq_dev * DH), BF16),
            pltpu.VMEM((NX, res_dev, 1024), F32),
            pltpu.VMEM((per, NY, res_dev, 1024), BF16),
            pltpu.VMEM((per, 3, res_dev, 1024), BF16),
            pltpu.VMEM((per, res_dev, 1024), F32),
            pltpu.VMEM((per, res_dev, 1024), BF16),
            pltpu.VMEM((per, res_dev, 1024), BF16),
            pltpu.VMEM((per, NY, res_dev, 1024), BF16),
            pltpu.VMEM((per, NX, res_dev, seq_dev * DH), BF16),
            pltpu.VMEM(block, BF16),
            pltpu.VMEM((rows, NX * DH), BF16),
            pltpu.VMEM((rows, width), F32),
            pltpu.SemaphoreType.DMA((10,)),
            pltpu.SemaphoreType.DMA((14, 5, 4)),
            pltpu.SemaphoreType.DMA((14, 5, 4)),
        ],
        cost_estimate=pl.CostEstimate(flops=6 * 10**9, bytes_accessed=10**7, transcendentals=2 * 10**5),
        compiler_params=pltpu.CompilerParams(
            collective_id=0, has_side_effects=True, vmem_limit_bytes=44 * 2**20
        ),
        name="tied_row_attention",
    )(tokens.reshape(rows, width), w_query, w_keyval, w_out.reshape(NX, per, DH, width))
    return mixed.reshape(seq_dev, res_dev, width)


def solution(mesh):
    return jax.shard_map(
        local,
        mesh=mesh,
        in_specs=(P("seq", "res", None), P(), P(), P()),
        out_specs=P("seq", "res", None),
        check_vma=False,
    )
```

time: 91.6 us -> 88.8 us (0.969)
  local copies, waits for them, and re-layouts: 0.01 us -> 6.88 us
  Pallas kernels: 86.8 us -> 81.3 us
  matrix products: 3.76 us -> 0 us
    unnamed x2 -> x9, local copies, waits for them, and re-layouts: 0.01 us -> 6.88 us
    pallas_call x1, Pallas kernels: 86.8 us -> 81.3 us  [local(): pl.pallas_call(functools.partial(layer_kernel, scale), out_shape=jax.Shap...]
    dot_general x1 -> x0, matrix products: 3.76 us -> none  [local(): mixed = jnp.dot(attended, w_out, preferred_element_type=F32)]
where the time goes in v2:
time: 88.8 us; the launch traced here: 88.2 us
  Pallas kernels  81.3 us (92%)
  local copies, waits for them, and re-layouts  6.88 us (8%)
    pallas_call x1, Pallas kernels, local(): pl.pallas_call(functools.partial(layer_kernel, scale), out_shape=jax.Shap...  81.3 us
    unnamed x9, local copies, waits for them, and re-layouts  6.88 us

profile of v2, /device:TPU:0, one launch (start us, length us, event | category | flops | bytes accessed | tf_op | source)
XLA Modules:
  0.0 88.2 jit_solution(14004984750325595164)
XLA Ops:
  0.0 0.0 copy-start
  0.0 1.7 %copy-done = bf16[768,1536]{1,0:T(8,128)(2,1)S(1)} copy-done((bf16[768,1536]{1,0:T(8,128)(2,1)S(1)}, bf16[768,1536]{1,0:T(8,128)(2,1)}, u32[]{:S(2)}) %copy-start) | copy-done | bytes 2359320
  1.7 0.0 copy-start.1
  1.7 1.3 %copy-done.1 = bf16[12,64,768]{2,1,0:T(8,128)(2,1)S(1)} copy-done((bf16[12,64,768]{2,1,0:T(8,128)(2,1)S(1)}, bf16[12,64,768]{2,1,0:T(8,128)(2,1)}, u32[]{:S(2)}) %copy-start.1) | copy-done | bytes 1179672
  2.9 0.0 copy-start.2
  2.9 1.3 %copy-done.2 = bf16[768,768]{1,0:T(8,128)(2,1)S(1)} copy-done((bf16[768,768]{1,0:T(8,128)(2,1)S(1)}, bf16[768,768]{1,0:T(8,128)(2,1)}, u32[]{:S(2)}) %copy-start.2) | copy-done | bytes 1179672
  4.2 0.0 copy-start.3
  4.2 1.3 %copy-done.3 = bf16[768,768]{1,0:T(8,128)(2,1)S(1)} copy-done((bf16[768,768]{1,0:T(8,128)(2,1)S(1)}, bf16[768,768]{1,0:T(8,128)(2,1)}, u32[]{:S(2)}) %copy-start.3) | copy-done | bytes 1179672
  5.5 81.3 %tied_row_attention.1 = f32[768,768]{1,0:T(8,128)S(1)} custom-call(bf16[768,768]{1,0:T(8,128)(2,1)S(1)} %bitcast.4, bf16[768,768]{1,0:T(8,128)(2,1)S(1)} %copy-done.2, bf16[768,1536]{1,0:T(8,128)(2,1)S(1)} %copy-done, bf16[4,3,64,768]{3,2,1,0:T(8,128)(2,1)S(1)} %bitcast.5), custom_call_target="tpu_custom_call" | custom-call | flops 6000000000 | bytes 10000000 | tf_op jit(solution)/shard_map/tied_row_attention/pallas_call | solution.py:329
  86.8 1.4 %copy.6 = f32[12,64,768]{2,1,0:T(8,128)} copy(f32[12,64,768]{2,1,0:T(8,128)S(1)} %bitcast.3) | data formatting | bytes 4718592
Async XLA Ops:
  0.0 1.7 %copy-start = (bf16[768,1536]{1,0:T(8,128)(2,1)S(1)}, bf16[768,1536]{1,0:T(8,128)(2,1)}, u32[]{:S(2)}) copy-start(bf16[768,1536]{1,0:T(8,128)(2,1)} %wkv_hbm.1) | copy-start | bytes 7077892
  1.7 1.3 %copy-start.1 = (bf16[12,64,768]{2,1,0:T(8,128)(2,1)S(1)}, bf16[12,64,768]{2,1,0:T(8,128)(2,1)}, u32[]{:S(2)}) copy-start(bf16[12,64,768]{2,1,0:T(8,128)(2,1)} %param.4) | copy-start | bytes 3538948
  2.9 1.3 %copy-start.2 = (bf16[768,768]{1,0:T(8,128)(2,1)S(1)}, bf16[768,768]{1,0:T(8,128)(2,1)}, u32[]{:S(2)}) copy-start(bf16[768,768]{1,0:T(8,128)(2,1)} %wq_hbm.1) | copy-start | bytes 3538948
  4.2 1.3 %copy-start.3 = (bf16[768,768]{1,0:T(8,128)(2,1)S(1)}, bf16[768,768]{1,0:T(8,128)(2,1)}, u32[]{:S(2)}) copy-start(bf16[768,768]{1,0:T(8,128)(2,1)} %param.7) | copy-start | bytes 3538948

commit v3 on v2

--- a/solution.py
+++ b/solution.py
@@ -42,7 +42,7 @@
 
     copies = {}
     seen = set()
-    slots = ["kx", "kz", "kc", "kt", "vx", "vz", "vc", "vt", "q", "r", "p", "a", "o", "t"]
+    slots = ["kx", "kz", "kc", "kt", "vx", "vz", "vc", "vt", "q", "r", "s", "p", "a", "b", "o", "t"]
 
     def send(kind, stage, k, src, dst, where):
         slot = slots.index(kind)
@@ -67,7 +67,7 @@
         pltpu.make_async_copy(wkv_hbm.at[:, pl.ds(0, half)], wkv.at[:, pl.ds(0, half)], load_sem.at[2]),
         pltpu.make_async_copy(wq_hbm, wq, load_sem.at[3]),
         pltpu.make_async_copy(wkv_hbm.at[:, pl.ds(half, half)], wkv.at[:, pl.ds(half, half)], load_sem.at[4]),
-    ] + [pltpu.make_async_copy(wout_hbm.at[:, hh], wout.at[hh], load_sem.at[5 + hh]) for hh in range(per)]
+    ] + [pltpu.make_async_copy(wout_hbm.at[:, hh], wout.at[0, hh], load_sem.at[5 + hh]) for hh in range(per)]
     for load in loads[:3]:
         load.start()
 
@@ -79,6 +79,9 @@
         load.start()
 
     low = lax.broadcasted_iota(jnp.int32, (64, 128), 1) < DH
+    lows = jnp.where(low, 1.0, 0.0).astype(BF16)
+    highs = jnp.where(low, 0.0, 1.0).astype(BF16)
+    stores = []
 
     def project(w, first, dst, factor=None, row=0, pairs=rows // 128):
         @pl.loop(0, width // COLS)
@@ -95,8 +98,8 @@
                     dst[head, :, m * 128:m * 128 + 128] = jnp.where(low, even, odd).astype(BF16)
                     dst[head + 1, :, m * 128:m * 128 + 128] = jnp.where(low, odd, even).astype(BF16)
 
-    mine = c * 2 + zl
-    theirs = c * 2 + (1 - zl)
+    mine = zl * 2 + c
+    theirs = (1 - zl) * 2 + c
     kv = {"k": (k_mine, k_all, k_more), "v": (v_mine, v_all, v_more)}
 
     def columns(stage):
@@ -158,43 +161,66 @@
             to = lax.rem(x + k, NX)
             send("q", hh, k, q_mine.at[per * to + hh], q_all.at[hh, x], at_x(k))
 
-    def logits(hh):
+    def logits(hh, half):
         arrived("q", hh, 2, 1, 3)
 
-        @pl.loop(0, 4)
+        @pl.loop(0, 2)
         def _(t):
             s = lax.dot_general(
-                q_all[hh].reshape(256, width), k_all[hh, t].reshape(256, width),
+                q_all[hh].reshape(256, width), k_all[hh, half * 2 + t].reshape(256, width),
                 (((1,), (1,)), ((), ())), preferred_element_type=F32,
             ).reshape(NX, 64, 256)
             at = pl.ds(pl.multiple_of(t * 256, 256), 256)
             scores[:, :, at] = s
-            part_out[hh, :, :, at] = s.astype(BF16)
-
-        own_rows[hh] = scores[y]
+            part_out[hh, half, :, :, at] = s.astype(BF16)
+
+        own_rows[hh, half] = scores[y]
+
+    def send_rows(kind, hh, half):
         for k in (2, 1, 3):
-            send("r", hh, k, part_out.at[hh, lax.rem(y + k, NY)], part_in.at[hh, k - 1], at_y(k))
+            send(kind, hh, k, part_out.at[hh, half, lax.rem(y + k, NY)], part_in.at[hh, half, k - 1], at_y(k))
+
+    def logits_mine(hh):
+        arrived("kc", hh, 0)
+        logits(hh, zl)
+        send_rows("s", hh, zl)
+
+    def logits_theirs(hh):
+        logits(hh, 1 - zl)
+        send_rows("r", hh, 1 - zl)
 
     def add_rows(hh):
+        arrived("s", hh, 2, 1, 3)
         arrived("r", hh, 2, 1, 3)
-        total = own_rows[hh]
-        for k in range(3):
-            total = total + part_in[hh, k].astype(F32)
-        own_rows[hh] = total
-        pair_out[hh] = total.astype(BF16)
+        for half in range(2):
+            total = own_rows[hh, half]
+            for k in range(3):
+                total = total + part_in[hh, half, k].astype(F32)
+            own_rows[hh, half] = total
+            pair_out[hh, half] = total.astype(BF16)
         send("p", hh, 0, pair_out.at[hh], pair_in.at[hh], at_zh)
 
     def softmax(hh):
         arrived("p", hh, 0)
-        total = own_rows[hh] + pair_in[hh].astype(F32)
-        weights = jnp.exp(total - jnp.max(total, axis=-1, keepdims=True))
-        probs[hh, y] = (weights / jnp.sum(weights, axis=-1, keepdims=True)).astype(BF16)
-        for k in (2, 1, 3):
+        totals = [own_rows[hh, half] + pair_in[hh, half].astype(F32) for half in range(2)]
+        largest = jnp.max(jnp.maximum(totals[0], totals[1]), axis=-1, keepdims=True)
+        weights = [jnp.exp(total - largest) for total in totals]
+        scaling = 1.0 / jnp.sum(weights[0] + weights[1], axis=-1, keepdims=True)
+        for half in range(2):
+            probs[hh, y, :, half * 512:half * 512 + 512] = (weights[half] * scaling).astype(BF16)
+        for k in (1, 3):
             send("a", hh, k, probs.at[hh, y], probs.at[hh, y], at_y(k))
+
+    def forward_probs(hh):
+        for k, first in ((1, 0), (3, 32)):
+            arrived("a", hh, k)
+            block = probs.at[hh, lax.rem(y + NY - k, NY), pl.ds(first, 32)]
+            send("b", hh, k, block, block, at_y(k))
 
     def attend(stage):
         hh, lo, n = columns(stage)
-        arrived("a", hh, 2, 1, 3)
+        arrived("a", hh, 1, 3)
+        arrived("b", hh, 1, 3)
 
         @pl.loop(lo // COLS, (lo + n) // COLS)
         def _(tile):
@@ -211,34 +237,42 @@
             to = lax.rem(x + k, NX)
             send("o", stage, k, att_out.at[hh, to, :, at], att_all.at[per * x + hh, :, at], at_x(k))
 
+    def swap_weights():
+        for load in loads[5:]:
+            load.wait()
+        for hh in range(per):
+            for xp in range(NX):
+                wout[1, hh, xp] = wout[0, hh, xp ^ 1]
+
     def project_out(stage):
         hh, lo, n = columns(stage)
         arrived("o", stage, 2, 1, 3)
-        if stage == 0:
-            for load in loads[5:]:
-                load.wait()
-        for m in range(lo // 128, (lo + n) // 128):
+        m0, m1 = lo // 128, (lo + n) // 128
+        for m in range(m0, m1):
             for pair in range(NX // 2):
-                a = att_all[2 * pair * per + hh, :, m * 128:m * 128 + 128].astype(F32)
-                b = att_all[(2 * pair + 1) * per + hh, :, m * 128:m * 128 + 128].astype(F32)
-                halves = [jnp.where(low, a, b), pltpu.roll(jnp.where(low, b, a), 64, 1)]
-                for s in range(2):
-                    left[m * 128 + s * 64:m * 128 + s * 64 + 64, pair * 128:pair * 128 + 128] = halves[
-                        (s + hh) % 2
-                    ].astype(BF16)
-        part = pl.ds(lo, n)
+                a = att_all[2 * pair * per + hh, :, m * 128:m * 128 + 128]
+                b = att_all[(2 * pair + 1) * per + hh, :, m * 128:m * 128 + 128]
+                left[0, m, :, pair * 128:pair * 128 + 128] = a * lows + b * highs
+                left[1, m, :, pair * 128:pair * 128 + 128] = b * lows + a * highs
 
         @pl.loop(0, width // COLS)
         def _(tile):
             at = pl.ds(pl.multiple_of(tile * COLS, COLS), COLS)
-            o = jnp.dot(left[part, :], wout[hh, :, :, at].reshape(NX * DH, COLS), preferred_element_type=F32)
-            mixed[part, at] = o if hh == 0 else mixed[part, at] + o
-
-    def store(stage):
-        _, lo, n = columns(stage)
-        copy = pltpu.make_async_copy(mixed.at[pl.ds(lo, n)], out_hbm.at[pl.ds(lo, n)], load_sem.at[5 + stage])
-        copy.start()
-        return copy
+            for q in range(2):
+                s = (hh + q) % 2
+                o = jnp.dot(
+                    left[q, m0:m1].reshape((m1 - m0) * 64, NX * DH), wout[q, hh, :, :, at].reshape(NX * DH, COLS),
+                    preferred_element_type=F32,
+                ).reshape(m1 - m0, 64, COLS)
+                mixed[s, m0:m1, :, at] = o if hh == 0 else mixed[s, m0:m1, :, at] + o
+        if hh == per - 1:
+            for s in range(2):
+                copy = pltpu.make_async_copy(
+                    mixed.at[s, pl.ds(m0, m1 - m0)], out_hbm.at[pl.ds(m0, m1 - m0), s],
+                    load_sem.at[5 + 2 * stage + s],
+                )
+                copy.start()
+                stores.append(copy)
 
     def start_tokens():
         loads[0].wait()
@@ -261,47 +295,54 @@
     start_tokens()
     project_keys()
     kv_send("k", 0)
+    project_values()
     kv_own("k", 0)
+    kv_send("k", 1)
+    project_query()
     kv_own("k", 1)
-    project_query()
-    kv_send("k", 1)
+    q_send(0)
+    kv_forward("k", 0)
     kv_more("k")
-    kv_forward("k", 0)
-    q_send(0)
+    kv_forward("k", 1)
+    kv_own("v", 0)
+    kv_own("k", 2)
+    q_send(1)
     kv_send("k", 2)
-    q_send(1)
-    kv_own("k", 2)
-    project_values()
+    logits_mine(0)
+    kv_own("v", 1)
+    kv_last("k", 0)
+    logits_theirs(0)
+    kv_last("k", 1)
+    kv_own("v", 3)
     q_send(2)
-    kv_forward("k", 1)
+    logits_mine(1)
+    logits_theirs(1)
+    kv_forward("k", 2)
+    add_rows(0)
     kv_send("v", 0)
+    kv_more("v")
     kv_send("v", 1)
-    kv_own("v", 4)
-    kv_last("k", 0)
-    logits(0)
+    swap_weights()
+    logits_mine(2)
+    add_rows(1)
+    kv_last("k", 2)
+    logits_theirs(2)
+    softmax(0)
+    kv_forward("v", 0)
     kv_send("v", 2)
-    kv_forward("k", 2)
-    kv_more("v")
-    kv_last("k", 1)
-    kv_own("v", 0)
-    logits(1)
-    add_rows(0)
-    kv_last("k", 2)
-    kv_own("v", 1)
-    logits(2)
-    kv_forward("v", 0)
-    softmax(0)
-    add_rows(1)
+    softmax(1)
     add_rows(2)
     kv_forward("v", 1)
+    forward_probs(0)
     kv_forward("v", 3)
-    softmax(1)
+    softmax(2)
+    kv_own("v", 4)
     kv_last("v", 0)
-    kv_own("v", 3)
-    softmax(2)
+    forward_probs(1)
     kv_forward("v", 4)
     attend(0)
     kv_last("v", 1)
+    forward_probs(2)
     attend(1)
     kv_last("v", 3)
     attend(3)
@@ -312,7 +353,6 @@
     project_out(3)
     project_out(4)
 
-    stores = [store(3), store(4)]
     for copy in copies.values():
         copy.wait_send()
     for copy in stores:
@@ -328,14 +368,14 @@
     block = (heads, res_dev, seq_dev * DH)
     mixed = pl.pallas_call(
         functools.partial(layer_kernel, scale),
-        out_shape=jax.ShapeDtypeStruct((rows, width), F32),
+        out_shape=jax.ShapeDtypeStruct((seq_dev // 2, 2, res_dev, width), F32),
         in_specs=[pl.BlockSpec(memory_space=pltpu.HBM)] * 4,
         out_specs=pl.BlockSpec(memory_space=pl.ANY),
         scratch_shapes=[
             pltpu.VMEM((rows + 128, width), BF16),
             pltpu.VMEM((width, width), BF16),
             pltpu.VMEM((width, 2 * width), BF16),
-            pltpu.VMEM((per, NX, DH, width), BF16),
+            pltpu.VMEM((2, per, NX, DH, width), BF16),
             pltpu.VMEM(block, BF16),
             pltpu.VMEM(block, BF16),
             pltpu.VMEM(block, BF16),
@@ -344,27 +384,27 @@
             pltpu.VMEM((per, NX, res_dev, seq_dev * DH), BF16),
             pltpu.VMEM((per, 4, NX, res_dev, seq_dev * DH), BF16),
             pltpu.VMEM((per, 4, NX, res_dev, seq_dev * DH), BF16),
-            pltpu.VMEM((NX, res_dev, 1024), F32),
-            pltpu.VMEM((per, NY, res_dev, 1024), BF16),
-            pltpu.VMEM((per, 3, res_dev, 1024), BF16),
-            pltpu.VMEM((per, res_dev, 1024), F32),
-            pltpu.VMEM((per, res_dev, 1024), BF16),
-            pltpu.VMEM((per, res_dev, 1024), BF16),
+            pltpu.VMEM((NX, res_dev, 512), F32),
+            pltpu.VMEM((per, 2, NY, res_dev, 512), BF16),
+            pltpu.VMEM((per, 2, 3, res_dev, 512), BF16),
+            pltpu.VMEM((per, 2, res_dev, 512), F32),
+            pltpu.VMEM((per, 2, res_dev, 512), BF16),
+            pltpu.VMEM((per, 2, res_dev, 512), BF16),
             pltpu.VMEM((per, NY, res_dev, 1024), BF16),
             pltpu.VMEM((per, NX, res_dev, seq_dev * DH), BF16),
             pltpu.VMEM(block, BF16),
-            pltpu.VMEM((rows, NX * DH), BF16),
-            pltpu.VMEM((rows, width), F32),
-            pltpu.SemaphoreType.DMA((10,)),
-            pltpu.SemaphoreType.DMA((14, 5, 4)),
-            pltpu.SemaphoreType.DMA((14, 5, 4)),
+            pltpu.VMEM((2, seq_dev // 2, res_dev, NX * DH), BF16),
+            pltpu.VMEM((2, seq_dev // 2, res_dev, width), F32),
+            pltpu.SemaphoreType.DMA((15,)),
+            pltpu.SemaphoreType.DMA((16, 5, 4)),
+            pltpu.SemaphoreType.DMA((16, 5, 4)),
         ],
         cost_estimate=pl.CostEstimate(flops=6 * 10**9, bytes_accessed=10**7, transcendentals=2 * 10**5),
         compiler_params=pltpu.CompilerParams(
             collective_id=0, has_side_effects=True, vmem_limit_bytes=44 * 2**20
         ),
         name="tied_row_attention",
-    )(tokens.reshape(rows, width), w_query, w_keyval, w_out.reshape(NX, per, DH, width))
+    )(*[pltpu.with_memory_space_constraint(a, pltpu.HBM) for a in (tokens.reshape(rows, width), w_query, w_keyval, w_out.reshape(NX, per, DH, width))])
     return mixed.reshape(seq_dev, res_dev, width)
 
 

time: 88.8 us -> 81.2 us (0.914)
  local copies, waits for them, and re-layouts: 6.88 us -> 1.41 us
  Pallas kernels: 81.3 us -> 78.7 us
    unnamed x9 -> x1, local copies, waits for them, and re-layouts: 6.88 us -> 1.41 us
    pallas_call x1, Pallas kernels: 81.3 us -> 78.7 us  [local(): pl.pallas_call(functools.partial(layer_kernel, scale), out_shape=jax.Shap...]
where the time goes in v3:
time: 81.2 us; the launch traced here: 80.1 us
  Pallas kernels  78.7 us (97%)
  local copies, waits for them, and re-layouts  1.41 us (2%)
    pallas_call x1, Pallas kernels, local(): pl.pallas_call(functools.partial(layer_kernel, scale), out_shape=jax.Shap...  78.7 us

profile of v3, /device:TPU:0, one launch (start us, length us, event | category | flops | bytes accessed | tf_op | source)
XLA Modules:
  0.0 80.1 jit_solution(9681344547038776114)
XLA Ops:
  0.0 78.7 %tied_row_attention.1 = f32[6,2,64,768]{3,2,1,0:T(8,128)S(1)} custom-call(bf16[768,768]{1,0:T(8,128)(2,1)} %bitcast.4, bf16[768,768]{1,0:T(8,128)(2,1)} %wq_hbm.1, bf16[768,1536]{1,0:T(8,128)(2,1)} %wkv_hbm.1, bf16[4,3,64,768]{3,2,1,0:T(8,128)(2,1)} %bitcast.5), custom_call_target="tpu_custom_call" | custom-call | flops 6000000000 | bytes 10000000 | tf_op jit(solution)/shard_map/tied_row_attention/pallas_call | solution.py:369
  78.7 1.4 %copy.6 = f32[12,64,768]{2,1,0:T(8,128)} copy(f32[12,64,768]{2,1,0:T(8,128)S(1)} %bitcast.3) | data formatting | bytes 4718592

commit v4 on v3

--- a/solution.py
+++ b/solution.py
@@ -18,9 +18,9 @@
 
 def layer_kernel(
     scale,
-    tok_hbm, wq_hbm, wkv_hbm, wout_hbm, out_hbm,
+    tok_hbm, wq_hbm, wkv_hbm, wout_ref, out_ref,
     tok, wq, wkv, wout, q_mine, k_mine, v_mine, k_more, v_more, q_all, k_all, v_all,
-    scores, part_out, part_in, own_rows, pair_out, pair_in, probs, att_out, att_all, left, mixed,
+    scores, part_out, part_in, own_rows, pair_out, pair_in, probs, att_out, att_all, left,
     load_sem, send_sem, recv_sem,
 ):
     seq, res = lax.axis_index("seq"), lax.axis_index("res")
@@ -42,16 +42,19 @@
 
     copies = {}
     seen = set()
-    slots = ["kx", "kz", "kc", "kt", "vx", "vz", "vc", "vt", "q", "r", "s", "p", "a", "b", "o", "t"]
-
-    def send(kind, stage, k, src, dst, where):
+    slots = ["kx", "kz", "kc", "kt", "vx", "vz", "vc", "vt", "q", "r", "s", "p", "u", "a", "e", "b", "o", "t"]
+
+    def send(kind, stage, k, src, dst, where, when=None):
         slot = slots.index(kind)
         copy = pltpu.make_async_remote_copy(
             src_ref=src, dst_ref=dst,
             send_sem=send_sem.at[slot, stage, k], recv_sem=recv_sem.at[slot, stage, k],
             device_id=where, device_id_type=MESH,
         )
-        copy.start()
+        if when is None:
+            copy.start()
+        else:
+            pl.when(when)(copy.start)
         copies[kind, stage, k] = copy
 
     def arrived(kind, stage, *ks):
@@ -67,7 +70,7 @@
         pltpu.make_async_copy(wkv_hbm.at[:, pl.ds(0, half)], wkv.at[:, pl.ds(0, half)], load_sem.at[2]),
         pltpu.make_async_copy(wq_hbm, wq, load_sem.at[3]),
         pltpu.make_async_copy(wkv_hbm.at[:, pl.ds(half, half)], wkv.at[:, pl.ds(half, half)], load_sem.at[4]),
-    ] + [pltpu.make_async_copy(wout_hbm.at[:, hh], wout.at[0, hh], load_sem.at[5 + hh]) for hh in range(per)]
+    ] + [pltpu.make_async_copy(wout_ref.at[:, hh], wout.at[0, hh], load_sem.at[5 + hh]) for hh in range(per)]
     for load in loads[:3]:
         load.start()
 
@@ -81,12 +84,10 @@
     low = lax.broadcasted_iota(jnp.int32, (64, 128), 1) < DH
     lows = jnp.where(low, 1.0, 0.0).astype(BF16)
     highs = jnp.where(low, 0.0, 1.0).astype(BF16)
-    stores = []
-
-    def project(w, first, dst, factor=None, row=0, pairs=rows // 128):
-        @pl.loop(0, width // COLS)
-        def _(n):
-            at = pl.multiple_of(first + n * COLS, COLS)
+
+    def project(w, first, dst, factor=None, row=0, pairs=rows // 128, after=None):
+        def tile(n):
+            at = first + n * COLS if after else pl.multiple_of(first + n * COLS, COLS)
             acc = jnp.dot(tok[row:row + pairs * 128], w[:, pl.ds(at, COLS)], preferred_element_type=F32)
             if factor is not None:
                 acc = acc * factor
@@ -97,6 +98,13 @@
                     head = n * (COLS // DH) + 2 * pair
                     dst[head, :, m * 128:m * 128 + 128] = jnp.where(low, even, odd).astype(BF16)
                     dst[head + 1, :, m * 128:m * 128 + 128] = jnp.where(low, odd, even).astype(BF16)
+
+        if after is None:
+            pl.loop(0, width // COLS)(tile)
+        else:
+            for n in range(width // COLS):
+                tile(n)
+                after(n)
 
     mine = zl * 2 + c
     theirs = (1 - zl) * 2 + c
@@ -189,27 +197,34 @@
         logits(hh, 1 - zl)
         send_rows("r", hh, 1 - zl)
 
-    def add_rows(hh):
-        arrived("s", hh, 2, 1, 3)
-        arrived("r", hh, 2, 1, 3)
-        for half in range(2):
-            total = own_rows[hh, half]
-            for k in range(3):
-                total = total + part_in[hh, half, k].astype(F32)
-            own_rows[hh, half] = total
-            pair_out[hh, half] = total.astype(BF16)
-        send("p", hh, 0, pair_out.at[hh], pair_in.at[hh], at_zh)
+    def add_rows(hh, kind, half, out):
+        arrived(kind, hh, 2, 1, 3)
+        total = own_rows[hh, half]
+        for k in range(3):
+            total = total + part_in[hh, half, k].astype(F32)
+        own_rows[hh, half] = total
+        pair_out[hh, half] = total.astype(BF16)
+        send(out, hh, 0, pair_out.at[hh, half], pair_in.at[hh, half], at_zh)
+
+    def add_mine(hh):
+        add_rows(hh, "s", zl, "p")
+
+    def add_theirs(hh):
+        add_rows(hh, "r", 1 - zl, "u")
 
     def softmax(hh):
         arrived("p", hh, 0)
+        arrived("u", hh, 0)
         totals = [own_rows[hh, half] + pair_in[hh, half].astype(F32) for half in range(2)]
         largest = jnp.max(jnp.maximum(totals[0], totals[1]), axis=-1, keepdims=True)
         weights = [jnp.exp(total - largest) for total in totals]
         scaling = 1.0 / jnp.sum(weights[0] + weights[1], axis=-1, keepdims=True)
         for half in range(2):
             probs[hh, y, :, half * 512:half * 512 + 512] = (weights[half] * scaling).astype(BF16)
-        for k in (1, 3):
-            send("a", hh, k, probs.at[hh, y], probs.at[hh, y], at_y(k))
+        for kind, first in (("a", 0), ("e", 32)):
+            for k in (1, 3):
+                block = probs.at[hh, y, pl.ds(first if k == 1 else 32 - first, 32)]
+                send(kind, hh, k, block, block, at_y(k))
 
     def forward_probs(hh):
         for k, first in ((1, 0), (3, 32)):
@@ -220,6 +235,7 @@
     def attend(stage):
         hh, lo, n = columns(stage)
         arrived("a", hh, 1, 3)
+        arrived("e", hh, 1, 3)
         arrived("b", hh, 1, 3)
 
         @pl.loop(lo // COLS, (lo + n) // COLS)
@@ -264,15 +280,22 @@
                     left[q, m0:m1].reshape((m1 - m0) * 64, NX * DH), wout[q, hh, :, :, at].reshape(NX * DH, COLS),
                     preferred_element_type=F32,
                 ).reshape(m1 - m0, 64, COLS)
-                mixed[s, m0:m1, :, at] = o if hh == 0 else mixed[s, m0:m1, :, at] + o
-        if hh == per - 1:
-            for s in range(2):
-                copy = pltpu.make_async_copy(
-                    mixed.at[s, pl.ds(m0, m1 - m0)], out_hbm.at[pl.ds(m0, m1 - m0), s],
-                    load_sem.at[5 + 2 * stage + s],
-                )
-                copy.start()
-                stores.append(copy)
+                out_ref[m0:m1, s, :, at] = o if hh == 0 else out_ref[m0:m1, s, :, at] + o
+
+    sent = set()
+
+    def drain(kinds=None, stages=range(5)):
+        for key, copy in copies.items():
+            if key not in sent and (kinds is None or key[0] in kinds) and key[1] in stages:
+                sent.add(key)
+                copy.wait_send()
+
+    def drain_keys():
+        drain(("t", "kx", "kz", "kc", "kt", "q", "r", "s"))
+
+    def drain_most():
+        drain(("vx", "vt", "p", "u"))
+        drain(("vz", "vc", "a", "e", "b", "o"), (0,))
 
     def start_tokens():
         loads[0].wait()
@@ -282,7 +305,16 @@
     def project_keys():
         loads[1].wait()
         loads[2].wait()
-        project(wkv, 0, k_mine)
+        src, dst, _ = kv["k"]
+
+        def after(n):
+            for k in (1, 3, 2):
+                to = lax.rem(x + k, NX)
+                ready = lax.div(per * to, COLS // DH) == n
+                send("kx", 0, k, src.at[per * to], dst.at[0, mine, x], at_x(k), ready)
+
+        project(wkv, 0, k_mine, after=after)
+        dst[0, mine, x] = src[per * x]
 
     def project_query():
         loads[3].wait()
@@ -294,56 +326,60 @@
 
     start_tokens()
     project_keys()
-    kv_send("k", 0)
+    kv_own("k", 1)
+    kv_send("k", 1)
+    kv_more("k")
+    kv_forward("k", 0)
+    project_query()
+    q_send(0)
+    q_send(1)
     project_values()
     kv_own("k", 0)
-    kv_send("k", 1)
-    project_query()
-    kv_own("k", 1)
-    q_send(0)
-    kv_forward("k", 0)
-    kv_more("k")
     kv_forward("k", 1)
     kv_own("v", 0)
+    kv_send("k", 2)
     kv_own("k", 2)
-    q_send(1)
-    kv_send("k", 2)
-    logits_mine(0)
+    q_send(2)
+    kv_send("v", 0)
+    kv_own("v", 4)
     kv_own("v", 1)
     kv_last("k", 0)
+    logits_mine(0)
     logits_theirs(0)
     kv_last("k", 1)
-    kv_own("v", 3)
-    q_send(2)
     logits_mine(1)
+    kv_send("v", 1)
+    kv_forward("k", 2)
     logits_theirs(1)
-    kv_forward("k", 2)
-    add_rows(0)
-    kv_send("v", 0)
     kv_more("v")
-    kv_send("v", 1)
-    swap_weights()
+    kv_send("v", 2)
+    add_mine(0)
+    add_theirs(0)
     logits_mine(2)
-    add_rows(1)
+    add_mine(1)
+    add_theirs(1)
     kv_last("k", 2)
     logits_theirs(2)
+    kv_forward("v", 0)
     softmax(0)
-    kv_forward("v", 0)
-    kv_send("v", 2)
     softmax(1)
-    add_rows(2)
+    add_mine(2)
+    add_theirs(2)
     kv_forward("v", 1)
+    kv_own("v", 3)
     forward_probs(0)
-    kv_forward("v", 3)
-    softmax(2)
-    kv_own("v", 4)
+    drain_keys()
     kv_last("v", 0)
     forward_probs(1)
+    softmax(2)
+    kv_forward("v", 3)
+    attend(0)
+    swap_weights()
     kv_forward("v", 4)
-    attend(0)
     kv_last("v", 1)
+    attend(1)
     forward_probs(2)
-    attend(1)
+    drain_most()
     kv_last("v", 3)
     attend(3)
     kv_last("v", 4)
@@ -353,10 +389,7 @@
     project_out(3)
     project_out(4)
 
-    for copy in copies.values():
-        copy.wait_send()
-    for copy in stores:
-        copy.wait()
+    drain()
 
 
 def local(tokens, w_query, w_keyval, w_out):
@@ -370,7 +403,7 @@
         functools.partial(layer_kernel, scale),
         out_shape=jax.ShapeDtypeStruct((seq_dev // 2, 2, res_dev, width), F32),
         in_specs=[pl.BlockSpec(memory_space=pltpu.HBM)] * 4,
-        out_specs=pl.BlockSpec(memory_space=pl.ANY),
+        out_specs=pl.BlockSpec(memory_space=pltpu.VMEM),
         scratch_shapes=[
             pltpu.VMEM((rows + 128, width), BF16),
             pltpu.VMEM((width, width), BF16),
@@ -394,10 +427,9 @@
             pltpu.VMEM((per, NX, res_dev, seq_dev * DH), BF16),
             pltpu.VMEM(block, BF16),
             pltpu.VMEM((2, seq_dev // 2, res_dev, NX * DH), BF16),
-            pltpu.VMEM((2, seq_dev // 2, res_dev, width), F32),
-            pltpu.SemaphoreType.DMA((15,)),
-            pltpu.SemaphoreType.DMA((16, 5, 4)),
-            pltpu.SemaphoreType.DMA((16, 5, 4)),
+            pltpu.SemaphoreType.DMA((8,)),
+            pltpu.SemaphoreType.DMA((18, 5, 4)),
+            pltpu.SemaphoreType.DMA((18, 5, 4)),
         ],
         cost_estimate=pl.CostEstimate(flops=6 * 10**9, bytes_accessed=10**7, transcendentals=2 * 10**5),
         compiler_params=pltpu.CompilerParams(

time: 81.2 us -> 81.5 us (level); the launches traced: 80.1 us -> 81.4 us
  Pallas kernels: 78.7 us -> 80 us
    pallas_call x1, Pallas kernels: 78.7 us -> 80 us  [local(): pl.pallas_call(functools.partial(layer_kernel, scale), out_shape=jax.Shap...]
where the time goes in v4:
time: 81.5 us; the launch traced here: 81.4 us
  Pallas kernels  80 us (98%)
  local copies, waits for them, and re-layouts  1.41 us (2%)
    pallas_call x1, Pallas kernels, local(): pl.pallas_call(functools.partial(layer_kernel, scale), out_shape=jax.Shap...  80 us

profile of v4, /device:TPU:0, one launch (start us, length us, event | category | flops | bytes accessed | tf_op | source)
XLA Modules:
  0.0 81.4 jit_solution(2195709501773016418)
XLA Ops:
  0.0 80.0 %tied_row_attention.1 = f32[6,2,64,768]{3,2,1,0:T(8,128)S(1)} custom-call(bf16[768,768]{1,0:T(8,128)(2,1)} %bitcast.4, bf16[768,768]{1,0:T(8,128)(2,1)} %wq_hbm.1, bf16[768,1536]{1,0:T(8,128)(2,1)} %wkv_hbm.1, bf16[4,3,64,768]{3,2,1,0:T(8,128)(2,1)} %bitcast.5), custom_call_target="tpu_custom_call" | custom-call | flops 6000000000 | bytes 10000000 | tf_op jit(solution)/shard_map/tied_row_attention/pallas_call | solution.py:402
  80.0 1.4 %copy.6 = f32[12,64,768]{2,1,0:T(8,128)} copy(f32[12,64,768]{2,1,0:T(8,128)S(1)} %bitcast.3) | data formatting | bytes 4718592

commit v5 on v4

--- a/solution.py
+++ b/solution.py
@@ -42,13 +42,13 @@
 
     copies = {}
     seen = set()
-    slots = ["kx", "kz", "kc", "kt", "vx", "vz", "vc", "vt", "q", "r", "s", "p", "u", "a", "e", "b", "o", "t"]
+    numbers = {}
 
     def send(kind, stage, k, src, dst, where, when=None):
-        slot = slots.index(kind)
+        number = numbers.setdefault((kind, stage, k), len(numbers))
         copy = pltpu.make_async_remote_copy(
             src_ref=src, dst_ref=dst,
-            send_sem=send_sem.at[slot, stage, k], recv_sem=recv_sem.at[slot, stage, k],
+            send_sem=send_sem.at[number], recv_sem=recv_sem.at[number],
             device_id=where, device_id_type=MESH,
         )
         if when is None:
@@ -428,8 +428,8 @@
             pltpu.VMEM(block, BF16),
             pltpu.VMEM((2, seq_dev // 2, res_dev, NX * DH), BF16),
             pltpu.SemaphoreType.DMA((8,)),
-            pltpu.SemaphoreType.DMA((18, 5, 4)),
-            pltpu.SemaphoreType.DMA((18, 5, 4)),
+            pltpu.SemaphoreType.DMA((132,)),
+            pltpu.SemaphoreType.DMA((132,)),
         ],
         cost_estimate=pl.CostEstimate(flops=6 * 10**9, bytes_accessed=10**7, transcendentals=2 * 10**5),
         compiler_params=pltpu.CompilerParams(

time: 81.5 us -> 77.4 us (0.950)
  Pallas kernels: 80 us -> 75.9 us
    pallas_call x1, Pallas kernels: 80 us -> 75.9 us  [local(): pl.pallas_call(functools.partial(layer_kernel, scale), out_shape=jax.Shap...]
where the time goes in v5:
time: 77.4 us; the launch traced here: 77.3 us
  Pallas kernels  75.9 us (98%)
  local copies, waits for them, and re-layouts  1.41 us (2%)
    pallas_call x1, Pallas kernels, local(): pl.pallas_call(functools.partial(layer_kernel, scale), out_shape=jax.Shap...  75.9 us

profile of v5, /device:TPU:0, one launch (start us, length us, event | category | flops | bytes accessed | tf_op | source)
XLA Modules:
  0.0 77.3 jit_solution(15964996929141570694)
XLA Ops:
  0.0 75.9 %tied_row_attention.1 = f32[6,2,64,768]{3,2,1,0:T(8,128)S(1)} custom-call(bf16[768,768]{1,0:T(8,128)(2,1)} %bitcast.4, bf16[768,768]{1,0:T(8,128)(2,1)} %wq_hbm.1, bf16[768,1536]{1,0:T(8,128)(2,1)} %wkv_hbm.1, bf16[4,3,64,768]{3,2,1,0:T(8,128)(2,1)} %bitcast.5), custom_call_target="tpu_custom_call" | custom-call | flops 6000000000 | bytes 10000000 | tf_op jit(solution)/shard_map/tied_row_attention/pallas_call | solution.py:402
  75.9 1.4 %copy.6 = f32[12,64,768]{2,1,0:T(8,128)} copy(f32[12,64,768]{2,1,0:T(8,128)S(1)} %bitcast.3) | data formatting | bytes 4718592

commit v6 on v5

--- a/solution.py
+++ b/solution.py
@@ -20,7 +20,7 @@
     scale,
     tok_hbm, wq_hbm, wkv_hbm, wout_ref, out_ref,
     tok, wq, wkv, wout, q_mine, k_mine, v_mine, k_more, v_more, q_all, k_all, v_all,
-    scores, part_out, part_in, own_rows, pair_out, pair_in, probs, att_out, att_all, left,
+    scores, part_out, part_in, own_rows, pair_out, pair_in, probs, att_out, att_all, lhs,
     load_sem, send_sem, recv_sem,
 ):
     seq, res = lax.axis_index("seq"), lax.axis_index("res")
@@ -40,28 +40,27 @@
     at_core = (seq, zl * 8 + x * 2 + (1 - c))
     at_zh = (y * 2 + (1 - zh), res)
 
-    copies = {}
-    seen = set()
-    numbers = {}
-
-    def send(kind, stage, k, src, dst, where, when=None):
-        number = numbers.setdefault((kind, stage, k), len(numbers))
+    senders, receivers, seen = {}, {}, set()
+
+    def send(kind, group, src, dst, where, when=None):
         copy = pltpu.make_async_remote_copy(
             src_ref=src, dst_ref=dst,
-            send_sem=send_sem.at[number], recv_sem=recv_sem.at[number],
+            send_sem=send_sem.at[senders.setdefault(kind, len(senders))],
+            recv_sem=recv_sem.at[receivers.setdefault(group, len(receivers))],
             device_id=where, device_id_type=MESH,
         )
         if when is None:
             copy.start()
         else:
             pl.when(when)(copy.start)
-        copies[kind, stage, k] = copy
-
-    def arrived(kind, stage, *ks):
-        for k in ks:
-            if (kind, stage, k) not in seen:
-                seen.add((kind, stage, k))
-                copies[kind, stage, k].wait_recv()
+
+    def arrived(group, ref):
+        if group not in seen:
+            seen.add(group)
+            pltpu.make_async_copy(ref, ref, recv_sem.at[receivers[group]]).wait()
+
+    def left(kind, ref):
+        pltpu.make_async_copy(ref, ref, send_sem.at[senders[kind]]).wait()
 
     half = wkv.shape[1] // 2
     loads = [
@@ -118,10 +117,11 @@
         dst[hh, mine, x] = src[per * x + hh]
         for k in (1, 3, 2):
             to = lax.rem(x + k, NX)
-            send(kind + "x", hh, k, src.at[per * to + hh], dst.at[hh, mine, x], at_x(k))
+            group = (kind + "x", hh, k if kind == "k" else 0)
+            send(kind + "x", group, src.at[per * to + hh], dst.at[hh, mine, x], at_x(k))
 
     def kv_more(kind):
-        arrived("t", 0, 0)
+        arrived("t", tok.at[pl.ds(rows, 128)])
         _, dst, src = kv[kind]
         project(wkv, 0 if kind == "k" else half, src, row=rows, pairs=1)
         for hh in range(per):
@@ -129,7 +129,7 @@
         for k in (2, 1, 3):
             to = lax.rem(x + k, NX)
             send(
-                kind + "t", 0, k, src.at[pl.ds(per * to, per)],
+                kind + "t", kind + "t", src.at[pl.ds(per * to, per)],
                 dst.at[pl.ds(0, per), theirs, x, :, pl.ds(0, MORE)], at_x(k),
             )
 
@@ -141,36 +141,47 @@
     def kv_own(kind, stage):
         src, dst, _ = kv[kind]
         hh, at = across(stage)
-        send(kind + "z", stage, 0, src.at[per * x + hh, :, at], dst.at[hh, mine, x, :, at], at_zl)
+        send(kind + "z", (kind + "z", stage), src.at[per * x + hh, :, at], dst.at[hh, mine, x, :, at], at_zl)
 
     def kv_forward(kind, stage):
         _, dst, _ = kv[kind]
         hh, at = across(stage)
         for k in (1, 3, 2):
-            arrived(kind + "x", hh, k)
-            block = dst.at[hh, mine, lax.rem(x + NX - k, NX), :, at]
-            send(kind + "z", stage, k, block, block, at_zl)
+            block = dst.at[hh, mine, lax.rem(x + NX - k, NX)]
+            if kind == "k":
+                arrived(("kx", hh, k), block)
+            else:
+                arrived(("vx", hh, 0), dst.at[hh, mine, pl.ds(0, 3)])
+            block = block.at[:, at]
+            send(kind + "z", (kind + "z", stage), block, block, at_zl)
         hh, lo, n = columns(stage)
         blocks = dst.at[hh, mine, :, :, pl.ds(lo, n)]
-        send(kind + "c", stage, 0, blocks, blocks, at_core)
+        send(kind + "c", (kind + "c", stage, 0), blocks, blocks, at_core)
 
     def kv_last(kind, stage):
         _, dst, _ = kv[kind]
-        arrived(kind + "t", 0, 2, 1, 3)
-        arrived(kind + "z", stage, 0, 1, 3, 2)
+        arrived(kind + "t", dst.at[pl.ds(0, per), theirs, pl.ds(0, 3), :, pl.ds(0, MORE)])
+        hh, at = across(stage)
+        arrived((kind + "z", stage), dst.at[hh, theirs, :, :, at])
         hh, lo, n = columns(stage)
-        blocks = dst.at[hh, theirs, :, :, pl.ds(lo, n)]
-        send(kind + "c", stage, 1, blocks, blocks, at_core)
-        arrived(kind + "c", stage, 0, 1)
+        at = pl.ds(lo, n)
+        blocks = dst.at[hh, theirs, :, :, at]
+        if kind == "k":
+            send("kc", ("kc", stage, 1), blocks, blocks, at_core)
+            arrived(("kc", stage, 0), dst.at[hh, 2 * zl + 1 - c])
+            arrived(("kc", stage, 1), dst.at[hh, 2 * (1 - zl) + 1 - c])
+        else:
+            send("vc", ("vc", stage, 0), blocks, blocks, at_core)
+            arrived(("vc", stage, 0), dst.at[hh, pl.ds(0, 2), :, :, at])
 
     def q_send(hh):
         q_all[hh, x] = q_mine[per * x + hh]
         for k in (2, 1, 3):
             to = lax.rem(x + k, NX)
-            send("q", hh, k, q_mine.at[per * to + hh], q_all.at[hh, x], at_x(k))
+            send("q", ("q", hh), q_mine.at[per * to + hh], q_all.at[hh, x], at_x(k))
 
     def logits(hh, half):
-        arrived("q", hh, 2, 1, 3)
+        arrived(("q", hh), q_all.at[hh, pl.ds(0, 3)])
 
         @pl.loop(0, 2)
         def _(t):
@@ -186,10 +197,12 @@
 
     def send_rows(kind, hh, half):
         for k in (2, 1, 3):
-            send(kind, hh, k, part_out.at[hh, half, lax.rem(y + k, NY)], part_in.at[hh, half, k - 1], at_y(k))
+            send(
+                kind, (kind, hh), part_out.at[hh, half, lax.rem(y + k, NY)], part_in.at[hh, half, k - 1], at_y(k)
+            )
 
     def logits_mine(hh):
-        arrived("kc", hh, 0)
+        arrived(("kc", hh, 0), k_all.at[hh, 2 * zl + 1 - c])
         logits(hh, zl)
         send_rows("s", hh, zl)
 
@@ -197,46 +210,44 @@
         logits(hh, 1 - zl)
         send_rows("r", hh, 1 - zl)
 
-    def add_rows(hh, kind, half, out):
-        arrived(kind, hh, 2, 1, 3)
+    def add_rows(hh, kind, half):
+        arrived((kind, hh), part_in.at[hh, half])
         total = own_rows[hh, half]
         for k in range(3):
             total = total + part_in[hh, half, k].astype(F32)
         own_rows[hh, half] = total
         pair_out[hh, half] = total.astype(BF16)
-        send(out, hh, 0, pair_out.at[hh, half], pair_in.at[hh, half], at_zh)
+        send("p", ("p", hh), pair_out.at[hh, half], pair_in.at[hh, half], at_zh)
 
     def add_mine(hh):
-        add_rows(hh, "s", zl, "p")
+        add_rows(hh, "s", zl)
 
     def add_theirs(hh):
-        add_rows(hh, "r", 1 - zl, "u")
+        add_rows(hh, "r", 1 - zl)
 
     def softmax(hh):
-        arrived("p", hh, 0)
-        arrived("u", hh, 0)
+        arrived(("p", hh), pair_in.at[hh])
         totals = [own_rows[hh, half] + pair_in[hh, half].astype(F32) for half in range(2)]
         largest = jnp.max(jnp.maximum(totals[0], totals[1]), axis=-1, keepdims=True)
         weights = [jnp.exp(total - largest) for total in totals]
         scaling = 1.0 / jnp.sum(weights[0] + weights[1], axis=-1, keepdims=True)
         for half in range(2):
             probs[hh, y, :, half * 512:half * 512 + 512] = (weights[half] * scaling).astype(BF16)
-        for kind, first in (("a", 0), ("e", 32)):
+        for kind, first in (("a", 0), ("b", 32)):
             for k in (1, 3):
                 block = probs.at[hh, y, pl.ds(first if k == 1 else 32 - first, 32)]
-                send(kind, hh, k, block, block, at_y(k))
+                send("a", (kind, hh), block, block, at_y(k))
 
     def forward_probs(hh):
         for k, first in ((1, 0), (3, 32)):
-            arrived("a", hh, k)
+            arrived(("a", hh), probs.at[hh, 0])
             block = probs.at[hh, lax.rem(y + NY - k, NY), pl.ds(first, 32)]
-            send("b", hh, k, block, block, at_y(k))
+            send("a", ("b", hh), block, block, at_y(k))
 
     def attend(stage):
         hh, lo, n = columns(stage)
-        arrived("a", hh, 1, 3)
-        arrived("e", hh, 1, 3)
-        arrived("b", hh, 1, 3)
+        arrived(("a", hh), probs.at[hh, 0])
+        arrived(("b", hh), probs.at[hh, pl.ds(0, 2)])
 
         @pl.loop(lo // COLS, (lo + n) // COLS)
         def _(tile):
@@ -251,7 +262,7 @@
         att_all[per * x + hh, :, at] = att_out[hh, x, :, at]
         for k in (2, 1, 3):
             to = lax.rem(x + k, NX)
-            send("o", stage, k, att_out.at[hh, to, :, at], att_all.at[per * x + hh, :, at], at_x(k))
+            send("o", ("o", stage), att_out.at[hh, to, :, at], att_all.at[per * x + hh, :, at], at_x(k))
 
     def swap_weights():
         for load in loads[5:]:
@@ -262,14 +273,14 @@
 
     def project_out(stage):
         hh, lo, n = columns(stage)
-        arrived("o", stage, 2, 1, 3)
+        arrived(("o", stage), att_all.at[pl.ds(0, 3), :, pl.ds(lo, n)])
         m0, m1 = lo // 128, (lo + n) // 128
         for m in range(m0, m1):
             for pair in range(NX // 2):
                 a = att_all[2 * pair * per + hh, :, m * 128:m * 128 + 128]
                 b = att_all[(2 * pair + 1) * per + hh, :, m * 128:m * 128 + 128]
-                left[0, m, :, pair * 128:pair * 128 + 128] = a * lows + b * highs
-                left[1, m, :, pair * 128:pair * 128 + 128] = b * lows + a * highs
+                lhs[0, m, :, pair * 128:pair * 128 + 128] = a * lows + b * highs
+                lhs[1, m, :, pair * 128:pair * 128 + 128] = b * lows + a * highs
 
         @pl.loop(0, width // COLS)
         def _(tile):
@@ -277,30 +288,37 @@
             for q in range(2):
                 s = (hh + q) % 2
                 o = jnp.dot(
-                    left[q, m0:m1].reshape((m1 - m0) * 64, NX * DH), wout[q, hh, :, :, at].reshape(NX * DH, COLS),
+                    lhs[q, m0:m1].reshape((m1 - m0) * 64, NX * DH), wout[q, hh, :, :, at].reshape(NX * DH, COLS),
                     preferred_element_type=F32,
                 ).reshape(m1 - m0, 64, COLS)
                 out_ref[m0:m1, s, :, at] = o if hh == 0 else out_ref[m0:m1, s, :, at] + o
 
-    sent = set()
-
-    def drain(kinds=None, stages=range(5)):
-        for key, copy in copies.items():
-            if key not in sent and (kinds is None or key[0] in kinds) and key[1] in stages:
-                sent.add(key)
-                copy.wait_send()
-
     def drain_keys():
-        drain(("t", "kx", "kz", "kc", "kt", "q", "r", "s"))
+        across_z = pl.ds(MORE, width - MORE)
+        left("t", tok.at[pl.ds(0, 128)])
+        left("kx", k_mine.at[pl.ds(0, 3 * per)])
+        left("kt", k_more.at[pl.ds(0, 3 * per)])
+        left("kz", k_mine.at[pl.ds(0, 4 * per), :, across_z])
+        left("kc", k_all.at[pl.ds(0, per), pl.ds(0, 2)])
+        left("q", q_mine.at[pl.ds(0, 3 * per)])
+        for kind in ("r", "s"):
+            left(kind, part_out.at[pl.ds(0, per), 0, pl.ds(0, 3)])
 
     def drain_most():
-        drain(("vx", "vt", "p", "u"))
-        drain(("vz", "vc", "a", "e", "b", "o"), (0,))
+        left("vx", v_mine.at[pl.ds(0, 3 * per)])
+        left("vt", v_more.at[pl.ds(0, 3 * per)])
+        left("p", pair_out)
+
+    def drain_last():
+        left("vz", v_mine.at[pl.ds(0, 4 * per), :, pl.ds(MORE, width - MORE)])
+        left("vc", v_all.at[pl.ds(0, per), pl.ds(0, 2)])
+        left("a", probs.at[pl.ds(0, per), pl.ds(0, 3)])
+        left("o", att_out.at[pl.ds(0, per), pl.ds(0, 3)])
 
     def start_tokens():
         loads[0].wait()
         pl.semaphore_wait(barrier, len(others))
-        send("t", 0, 0, tok.at[pl.ds(0, 128)], tok.at[pl.ds(rows, 128)], at_zl)
+        send("t", "t", tok.at[pl.ds(0, 128)], tok.at[pl.ds(rows, 128)], at_zl)
 
     def project_keys():
         loads[1].wait()
@@ -311,7 +329,7 @@
             for k in (1, 3, 2):
                 to = lax.rem(x + k, NX)
                 ready = lax.div(per * to, COLS // DH) == n
-                send("kx", 0, k, src.at[per * to], dst.at[0, mine, x], at_x(k), ready)
+                send("kx", ("kx", 0, k), src.at[per * to], dst.at[0, mine, x], at_x(k), ready)
 
         project(wkv, 0, k_mine, after=after)
         dst[0, mine, x] = src[per * x]
@@ -389,7 +407,7 @@
     project_out(3)
     project_out(4)
 
-    drain()
+    drain_last()
 
 
 def local(tokens, w_query, w_keyval, w_out):
@@ -428,8 +446,8 @@
             pltpu.VMEM(block, BF16),
             pltpu.VMEM((2, seq_dev // 2, res_dev, NX * DH), BF16),
             pltpu.SemaphoreType.DMA((8,)),
-            pltpu.SemaphoreType.DMA((132,)),
-            pltpu.SemaphoreType.DMA((132,)),
+            pltpu.SemaphoreType.DMA((15,)),
+            pltpu.SemaphoreType.DMA((54,)),
         ],
         cost_estimate=pl.CostEstimate(flops=6 * 10**9, bytes_accessed=10**7, transcendentals=2 * 10**5),
         compiler_params=pltpu.CompilerParams(

time: 77.4 us -> 75.6 us (0.977)
  Pallas kernels: 75.9 us -> 74.1 us
    pallas_call x1, Pallas kernels: 75.9 us -> 74.1 us  [local(): pl.pallas_call(functools.partial(layer_kernel, scale), out_shape=jax.Shap...]
where the time goes in v6:
time: 75.6 us; the launch traced here: 75.5 us
  Pallas kernels  74.1 us (98%)
  local copies, waits for them, and re-layouts  1.41 us (2%)
    pallas_call x1, Pallas kernels, local(): pl.pallas_call(functools.partial(layer_kernel, scale), out_shape=jax.Shap...  74.1 us

profile of v6, /device:TPU:0, one launch (start us, length us, event | category | flops | bytes accessed | tf_op | source)
XLA Modules:
  0.0 75.5 jit_solution(7262263826399240391)
XLA Ops:
  0.0 74.1 %tied_row_attention.1 = f32[6,2,64,768]{3,2,1,0:T(8,128)S(1)} custom-call(bf16[768,768]{1,0:T(8,128)(2,1)} %bitcast.4, bf16[768,768]{1,0:T(8,128)(2,1)} %wq_hbm.1, bf16[768,1536]{1,0:T(8,128)(2,1)} %wkv_hbm.1, bf16[4,3,64,768]{3,2,1,0:T(8,128)(2,1)} %bitcast.5), custom_call_target="tpu_custom_call" | custom-call | flops 6000000000 | bytes 10000000 | tf_op jit(solution)/shard_map/tied_row_attention/pallas_call | solution.py:420
  74.1 1.4 %copy.6 = f32[12,64,768]{2,1,0:T(8,128)} copy(f32[12,64,768]{2,1,0:T(8,128)S(1)} %bitcast.3) | data formatting | bytes 4718592

commit v7 on v6

--- a/solution.py
+++ b/solution.py
@@ -344,59 +344,59 @@
 
     start_tokens()
     project_keys()
-    kv_own("k", 1)
-    kv_send("k", 1)
-    kv_more("k")
-    kv_forward("k", 0)
+    kv_own("k", 0)
     project_query()
     q_send(0)
+    project_values()
+    kv_own("k", 2)
+    kv_send("k", 1)
+    kv_own("k", 1)
+    kv_more("k")
     q_send(1)
-    project_values()
-    kv_own("k", 0)
+    kv_forward("k", 0)
+    kv_send("k", 2)
     kv_forward("k", 1)
+    logits_mine(0)
+    kv_own("v", 1)
+    q_send(2)
+    kv_last("k", 0)
     kv_own("v", 0)
-    kv_send("k", 2)
-    kv_own("k", 2)
-    q_send(2)
+    logits_theirs(0)
+    add_mine(0)
     kv_send("v", 0)
-    kv_own("v", 4)
-    kv_own("v", 1)
-    kv_last("k", 0)
-    logits_mine(0)
-    logits_theirs(0)
+    logits_mine(1)
     kv_last("k", 1)
-    logits_mine(1)
+    kv_forward("k", 2)
+    add_theirs(0)
+    logits_theirs(1)
     kv_send("v", 1)
-    kv_forward("k", 2)
-    logits_theirs(1)
     kv_more("v")
-    kv_send("v", 2)
-    add_mine(0)
-    add_theirs(0)
     logits_mine(2)
     add_mine(1)
+    swap_weights()
     add_theirs(1)
     kv_last("k", 2)
+    kv_forward("v", 0)
     logits_theirs(2)
-    kv_forward("v", 0)
+    drain_keys()
     softmax(0)
-    softmax(1)
+    kv_send("v", 2)
     add_mine(2)
     add_theirs(2)
+    softmax(1)
     kv_forward("v", 1)
-    kv_own("v", 3)
     forward_probs(0)
-    drain_keys()
     kv_last("v", 0)
     forward_probs(1)
+    kv_forward("v", 3)
+    kv_own("v", 3)
+    kv_own("v", 4)
+    kv_forward("v", 4)
     softmax(2)
-    kv_forward("v", 3)
     attend(0)
-    swap_weights()
-    kv_forward("v", 4)
     kv_last("v", 1)
+    forward_probs(2)
     attend(1)
-    forward_probs(2)
     drain_most()
     kv_last("v", 3)
     attend(3)

time: 75.6 us -> 75.2 us (level)
  Pallas kernels: 74.1 us -> 73.3 us
    pallas_call x1, Pallas kernels: 74.1 us -> 73.3 us  [local(): pl.pallas_call(functools.partial(layer_kernel, scale), out_shape=jax.Shap...]
where the time goes in v7:
time: 75.2 us; the launch traced here: 74.7 us
  Pallas kernels  73.3 us (97%)
  local copies, waits for them, and re-layouts  1.41 us (2%)
    pallas_call x1, Pallas kernels, local(): pl.pallas_call(functools.partial(layer_kernel, scale), out_shape=jax.Shap...  73.3 us

profile of v7, /device:TPU:0, one launch (start us, length us, event | category | flops | bytes accessed | tf_op | source)
XLA Modules:
  0.0 74.7 jit_solution(10300376088888493016)
XLA Ops:
  0.0 73.3 %tied_row_attention.1 = f32[6,2,64,768]{3,2,1,0:T(8,128)S(1)} custom-call(bf16[768,768]{1,0:T(8,128)(2,1)} %bitcast.4, bf16[768,768]{1,0:T(8,128)(2,1)} %wq_hbm.1, bf16[768,1536]{1,0:T(8,128)(2,1)} %wkv_hbm.1, bf16[4,3,64,768]{3,2,1,0:T(8,128)(2,1)} %bitcast.5), custom_call_target="tpu_custom_call" | custom-call | flops 6000000000 | bytes 10000000 | tf_op jit(solution)/shard_map/tied_row_attention/pallas_call | solution.py:420
  73.3 1.4 %copy.6 = f32[12,64,768]{2,1,0:T(8,128)} copy(f32[12,64,768]{2,1,0:T(8,128)S(1)} %bitcast.3) | data formatting | bytes 4718592

commit v8 on v7

--- a/solution.py
+++ b/solution.py
@@ -65,8 +65,8 @@
     half = wkv.shape[1] // 2
     loads = [
         pltpu.make_async_copy(tok_hbm.at[pl.ds(0, 128)], tok.at[pl.ds(0, 128)], load_sem.at[0]),
-        pltpu.make_async_copy(tok_hbm.at[pl.ds(128, rows - 128)], tok.at[pl.ds(128, rows - 128)], load_sem.at[1]),
-        pltpu.make_async_copy(wkv_hbm.at[:, pl.ds(0, half)], wkv.at[:, pl.ds(0, half)], load_sem.at[2]),
+        pltpu.make_async_copy(wkv_hbm.at[:, pl.ds(0, half)], wkv.at[:, pl.ds(0, half)], load_sem.at[1]),
+        pltpu.make_async_copy(tok_hbm.at[pl.ds(128, rows - 128)], tok.at[pl.ds(128, rows - 128)], load_sem.at[2]),
         pltpu.make_async_copy(wq_hbm, wq, load_sem.at[3]),
         pltpu.make_async_copy(wkv_hbm.at[:, pl.ds(half, half)], wkv.at[:, pl.ds(half, half)], load_sem.at[4]),
     ] + [pltpu.make_async_copy(wout_ref.at[:, hh], wout.at[0, hh], load_sem.at[5 + hh]) for hh in range(per)]
@@ -323,16 +323,8 @@
     def project_keys():
         loads[1].wait()
         loads[2].wait()
-        src, dst, _ = kv["k"]
-
-        def after(n):
-            for k in (1, 3, 2):
-                to = lax.rem(x + k, NX)
-                ready = lax.div(per * to, COLS // DH) == n
-                send("kx", ("kx", 0, k), src.at[per * to], dst.at[0, mine, x], at_x(k), ready)
-
-        project(wkv, 0, k_mine, after=after)
-        dst[0, mine, x] = src[per * x]
+        project(wkv, 0, k_mine)
+        kv_send("k", 0)
 
     def project_query():
         loads[3].wait()

time: 75.2 us -> 75 us (level)
  no operation moved by 1% of the time
where the time goes in v8:
time: 75 us; the launch traced here: 74.9 us
  Pallas kernels  73.5 us (98%)
  local copies, waits for them, and re-layouts  1.41 us (2%)
    pallas_call x1, Pallas kernels, local(): pl.pallas_call(functools.partial(layer_kernel, scale), out_shape=jax.Shap...  73.5 us

profile of v8, /device:TPU:0, one launch (start us, length us, event | category | flops | bytes accessed | tf_op | source)
XLA Modules:
  0.0 74.9 jit_solution(16327684798382603117)
XLA Ops:
  0.0 73.5 %tied_row_attention.1 = f32[6,2,64,768]{3,2,1,0:T(8,128)S(1)} custom-call(bf16[768,768]{1,0:T(8,128)(2,1)} %bitcast.4, bf16[768,768]{1,0:T(8,128)(2,1)} %wq_hbm.1, bf16[768,1536]{1,0:T(8,128)(2,1)} %wkv_hbm.1, bf16[4,3,64,768]{3,2,1,0:T(8,128)(2,1)} %bitcast.5), custom_call_target="tpu_custom_call" | custom-call | flops 6000000000 | bytes 10000000 | tf_op jit(solution)/shard_map/tied_row_attention/pallas_call | solution.py:412
  73.5 1.4 %copy.6 = f32[12,64,768]{2,1,0:T(8,128)} copy(f32[12,64,768]{2,1,0:T(8,128)S(1)} %bitcast.3) | data formatting | bytes 4718592

commit v9 on v8

--- a/solution.py
+++ b/solution.py
@@ -65,8 +65,8 @@
     half = wkv.shape[1] // 2
     loads = [
         pltpu.make_async_copy(tok_hbm.at[pl.ds(0, 128)], tok.at[pl.ds(0, 128)], load_sem.at[0]),
-        pltpu.make_async_copy(wkv_hbm.at[:, pl.ds(0, half)], wkv.at[:, pl.ds(0, half)], load_sem.at[1]),
-        pltpu.make_async_copy(tok_hbm.at[pl.ds(128, rows - 128)], tok.at[pl.ds(128, rows - 128)], load_sem.at[2]),
+        pltpu.make_async_copy(tok_hbm.at[pl.ds(128, rows - 128)], tok.at[pl.ds(128, rows - 128)], load_sem.at[1]),
+        pltpu.make_async_copy(wkv_hbm.at[:, pl.ds(0, half)], wkv.at[:, pl.ds(0, half)], load_sem.at[2]),
         pltpu.make_async_copy(wq_hbm, wq, load_sem.at[3]),
         pltpu.make_async_copy(wkv_hbm.at[:, pl.ds(half, half)], wkv.at[:, pl.ds(half, half)], load_sem.at[4]),
     ] + [pltpu.make_async_copy(wout_ref.at[:, hh], wout.at[0, hh], load_sem.at[5 + hh]) for hh in range(per)]

time: 75 us -> 75 us (level)
  no operation moved by 1% of the time
where the time goes in v9:
time: 75 us; the launch traced here: 74.9 us
  Pallas kernels  73.5 us (98%)
  local copies, waits for them, and re-layouts  1.41 us (2%)
    pallas_call x1, Pallas kernels, local(): pl.pallas_call(functools.partial(layer_kernel, scale), out_shape=jax.Shap...  73.5 us

profile of v9, /device:TPU:0, one launch (start us, length us, event | category | flops | bytes accessed | tf_op | source)
XLA Modules:
  0.0 74.9 jit_solution(18013143223566245023)
XLA Ops:
  0.0 73.5 %tied_row_attention.1 = f32[6,2,64,768]{3,2,1,0:T(8,128)S(1)} custom-call(bf16[768,768]{1,0:T(8,128)(2,1)} %bitcast.4, bf16[768,768]{1,0:T(8,128)(2,1)} %wq_hbm.1, bf16[768,1536]{1,0:T(8,128)(2,1)} %wkv_hbm.1, bf16[4,3,64,768]{3,2,1,0:T(8,128)(2,1)} %bitcast.5), custom_call_target="tpu_custom_call" | custom-call | flops 6000000000 | bytes 10000000 | tf_op jit(solution)/shard_map/tied_row_attention/pallas_call | solution.py:412
  73.5 1.4 %copy.6 = f32[12,64,768]{2,1,0:T(8,128)} copy(f32[12,64,768]{2,1,0:T(8,128)S(1)} %bitcast.3) | data formatting | bytes 4718592
